TPU v7x, 1024 devices: a whole 4x8x16 slice. The times are simulated.
1024 devices in a mesh: node: 16 (over z), local: 64 (over y, x, core).
Axes of the slice: x: 4, y: 8, z: 16, core: 2. Of those that a mesh axis runs over, the one named last changes fastest.
Arguments:
- tokens: bfloat16 [1024, 3584], P(('node', 'local')), may hold values from -6 to 6
- out_grad: bfloat16 [1024, 3584], P(('node', 'local')), may hold values from -2 to 2
- gate_prob: bfloat16 [1024, 8], P(('node', 'local')), may hold values from 0.099609375 to 1
- dest_node: int32 [1024, 8], P(('node', 'local')), may hold values from 0 to 15, as said below
- w_gate: bfloat16 [1024, 3584, 128], P(('node', 'local')), may hold values from -0.09375 to 0.09375
- w_up: bfloat16 [1024, 3584, 128], P(('node', 'local')), may hold values from -0.09375 to 0.09375
- w_down: bfloat16 [1024, 128, 3584], P(('node', 'local')), may hold values from -0.1875 to 0.1875
Outputs:
- in_grad: bfloat16 [1024, 3584], P(('node', 'local'))
- gate_grad: float32 [1024, 8], P(('node', 'local'))
Inputs may be any that keep to these rules, and one draw needn't show every extreme that they name: `dest_node`: columns 2 * g and 2 * g + 1 of a row are equal, so a token names at most half of 8 node groups, two experts in each. Among the 64 tokens of one node group, at most 8 name the same node group in one column; for each pair of columns one node group, the same for all source groups, is named by exactly 8 of them.
All inputs are finite; a program needn't handle non-finite values.
Results may differ from a plain program's by a relative error of at most 0.006.
Values may be sent and summed in bfloat16 or wider, within the bound.
No kernel may reach another device: no remote copies, remote signals or barrier semaphores. Data moves between devices by JAX's collectives and lax.ppermute only.
A program may use at most 32 MiB of HBM per device.

v0:
```python
import jax
import jax.numpy as jnp
from jax import lax
from jax.sharding import PartitionSpec as P


def expert_terms(rows_x, rows_dy, rows_gate, weight_gate, weight_up, weight_down):
    contract = (((1,), (1,)), ((), ()))
    pre_gate = jnp.dot(rows_x, weight_gate, preferred_element_type=jnp.float32)
    pre_up = jnp.dot(rows_x, weight_up, preferred_element_type=jnp.float32)
    logistic = jax.nn.sigmoid(pre_gate)
    swished = pre_gate * logistic
    hidden = swished * pre_up
    back_hidden = lax.dot_general(
        rows_dy, weight_down, contract, preferred_element_type=jnp.float32
    )
    gate_terms = jnp.sum(hidden * back_hidden, axis=1)
    scaled = rows_gate[:, None] * back_hidden
    grad_gate = (scaled * pre_up * logistic * (1.0 + pre_gate * (1.0 - logistic))).astype(
        jnp.bfloat16
    )
    grad_up = (scaled * swished).astype(jnp.bfloat16)
    input_terms = lax.dot_general(
        grad_gate, weight_gate, contract, preferred_element_type=jnp.float32
    )
    input_terms = input_terms + lax.dot_general(
        grad_up, weight_up, contract, preferred_element_type=jnp.float32
    )
    return (input_terms, gate_terms)


def on_device(tokens, out_grad, gate_prob, dest_node, w_gate, w_up, w_down):
    node_count = lax.axis_size("node")
    local_count = lax.axis_size("local")
    local_id = lax.axis_index("local")
    width = tokens.shape[1]
    experts_here = gate_prob.shape[1]
    shards = local_count // experts_here
    column = local_id // shards
    pick_float = (jnp.arange(experts_here) == column).astype(jnp.float32)
    dest_half = dest_node.astype(jnp.bfloat16)
    home_x, home_dy, home_gate, home_dest = (
        lax.all_gather(tokens, "local", axis=0, tiled=True),
        lax.all_gather(out_grad, "local", axis=0, tiled=True),
        lax.all_gather(gate_prob, "local", axis=0, tiled=True),
        lax.all_gather(dest_half, "local", axis=0, tiled=True),
    )
    members = home_x.shape[0]
    capacity = 2 * members // node_count
    slots = node_count * capacity
    target = jnp.sum(home_dest.astype(jnp.float32) * pick_float[None, :], axis=1).astype(jnp.int32)
    onehot_dest = (target[:, None] == jnp.arange(node_count)[None, :]).astype(jnp.int32)
    before = jnp.cumsum(onehot_dest, axis=0) - onehot_dest
    position = target * capacity + jnp.sum(before * onehot_dest, axis=1)
    place_half = (jnp.arange(slots)[:, None] == position[None, :]).astype(jnp.bfloat16)
    send_x = jnp.dot(place_half, home_x, preferred_element_type=jnp.float32).astype(jnp.bfloat16)
    send_dy = jnp.dot(place_half, home_dy, preferred_element_type=jnp.float32).astype(jnp.bfloat16)
    send_gate = jnp.dot(place_half, home_gate, preferred_element_type=jnp.float32).astype(
        jnp.bfloat16
    )
    weight_gate = w_gate[0]
    weight_up = w_up[0]
    weight_down = w_down[0]
    part_x = lax.all_to_all(
        send_x.reshape(node_count, capacity, width), "node", split_axis=0, concat_axis=0, tiled=True
    )
    part_dy = lax.all_to_all(
        send_dy.reshape(node_count, capacity, width),
        "node",
        split_axis=0,
        concat_axis=0,
        tiled=True,
    )
    part_gate = lax.all_to_all(
        send_gate.reshape(node_count, capacity, experts_here),
        "node",
        split_axis=0,
        concat_axis=0,
        tiled=True,
    )
    leading = part_x.shape[0]
    items = part_x.shape[1]
    count = leading * items
    rows_gate = jnp.sum(
        part_gate.reshape(count, experts_here).astype(jnp.float32) * pick_float[None, :], axis=1
    )
    input_terms, gate_terms = expert_terms(
        part_x.reshape(count, width),
        part_dy.reshape(count, width),
        rows_gate,
        weight_gate,
        weight_up,
        weight_down,
    )
    gate_cols = gate_terms[:, None] * pick_float[None, :]
    back_x = lax.all_to_all(
        input_terms.reshape(leading, items, width), "node", split_axis=0, concat_axis=0, tiled=True
    )
    back_gate = lax.all_to_all(
        gate_cols.reshape(leading, items, experts_here),
        "node",
        split_axis=0,
        concat_axis=0,
        tiled=True,
    )
    term_x = jnp.take(back_x.reshape(slots, width), position, axis=0)
    term_gate = jnp.take(back_gate.reshape(slots, experts_here), position, axis=0)
    summed_x, summed_gate = (
        lax.psum_scatter(term_x, "local", scatter_dimension=0, tiled=True),
        lax.psum_scatter(term_gate, "local", scatter_dimension=0, tiled=True),
    )
    return (summed_x.astype(jnp.bfloat16), summed_gate)


def solution(mesh):
    return jax.shard_map(
        on_device,
        mesh=mesh,
        in_specs=(
            P(("node", "local"), None),
            P(("node", "local"), None),
            P(("node", "local"), None),
            P(("node", "local"), None),
            P(("node", "local"), None, None),
            P(("node", "local"), None, None),
            P(("node", "local"), None, None),
        ),
        out_specs=(P(("node", "local"), None), P(("node", "local"), None)),
        check_vma=False,
    )
```

profile of v0, /device:TPU:1, one launch (start us, length us, event | category | flops | bytes accessed | tf_op | source)
XLA Modules:
  0.0 593.3 jit_solution(8299669261612920272)
XLA Ops:
  0.7 0.7 convert_bitcast_fusion
  1.4 46.9 %all-gather = bf16[64,1,8]{2,1,0:T(2,128)(2,1)S(1)} all-gather(bf16[1,1,8]{2,1,0:T(2,128)(2,1)S(1)} %convert_bitcast_fusion), channel_id=1, replica_groups=mesh['node'=16,'local'=64] {'local'}, dimensions={0}, use_global_device_ids=true | all-gather | bytes 1040 | tf_op jit(solution)/shard_map/all_gather | solution.py:46
  48.7 0.2 select_reduce_fusion
  48.9 48.7 %all-gather.3 = bf16[64,1,3584]{2,1,0:T(2,128)(2,1)S(1)} all-gather(bf16[1,1,3584]{2,1,0:T(2,128)(2,1)} %bitcast.58), channel_id=1, replica_groups=mesh['node'=16,'local'=64] {'local'}, dimensions={0}, use_global_device_ids=true | all-gather | bytes 465920 | tf_op jit(solution)/shard_map/all_gather | solution.py:43
  97.6 1.4 fusion.2
  98.9 10.1 %all-to-all-start.2 = ((bf16[16,8,3584]{2,1,0:T(8,128)(2,1)}), bf16[16,8,3584]{2,1,0:T(8,128)(2,1)S(1)}, u32[]{:S(2)}, u32[]{:S(2)}) async-start(bf16[16,8,3584]{2,1,0:T(8,128)(2,1)} %fusion.2), calls=%async_computation.2 | async-start | bytes 1835008 | tf_op jit(solution)/shard_map/all_to_all | solution.py:64
  109.1 49.2 %all-gather.2 = bf16[64,1,3584]{2,1,0:T(2,128)(2,1)S(1)} all-gather(bf16[1,1,3584]{2,1,0:T(2,128)(2,1)S(1)} %bitcast.59), channel_id=1, replica_groups=mesh['node'=16,'local'=64] {'local'}, dimensions={0}, use_global_device_ids=true | all-gather | bytes 465920 | tf_op jit(solution)/shard_map/all_gather | solution.py:44
  158.3 1.3 fusion.1
  159.6 11.9 %all-to-all-start.1 = ((bf16[16,8,3584]{2,1,0:T(8,128)(2,1)}), bf16[16,8,3584]{2,1,0:T(8,128)(2,1)}, u32[]{:S(2)}, u32[]{:S(2)}) async-start(bf16[16,8,3584]{2,1,0:T(8,128)(2,1)} %fusion.1), calls=%async_computation.1 | async-start | bytes 1835008 | tf_op jit(solution)/shard_map/all_to_all | solution.py:67
  171.6 33.3 %all-gather.1 = bf16[64,1,8]{2,1,0:T(2,128)(2,1)S(1)} all-gather(bf16[1,1,8]{2,1,0:T(2,128)(2,1)S(1)} %bitcast.60), channel_id=1, replica_groups=mesh['node'=16,'local'=64] {'local'}, dimensions={0}, use_global_device_ids=true | all-gather | bytes 1040 | tf_op jit(solution)/shard_map/all_gather | solution.py:45
  204.9 0.1 convolution_convert_fusion.2
  205.2 0.6 copy.13
  205.8 0.5 fusion.5
  206.3 0.5 fusion.8
  206.8 6.4 %all-to-all-done.1 = bf16[16,8,3584]{2,1,0:T(8,128)(2,1)} async-done(((bf16[16,8,3584]{2,1,0:T(8,128)(2,1)}), bf16[16,8,3584]{2,1,0:T(8,128)(2,1)}, u32[]{:S(2)}, u32[]{:S(2)}) %all-to-all-start.1) | async-done | bytes 917536 | tf_op jit(solution)/shard_map/all_to_all | solution.py:67
  213.2 10.8 %all-to-all-start = ((bf16[16,8,8]{1,2,0:T(8,128)(2,1)}), bf16[16,8,8]{1,2,0:T(8,128)(2,1)S(1)}, u32[]{:S(2)}, u32[]{:S(2)}) async-start(bf16[16,8,8]{1,2,0:T(8,128)(2,1)} %copy.13), calls=%async_computation | async-start | bytes 65536 | tf_op jit(solution)/shard_map/all_to_all | solution.py:74
  224.0 1.9 multiply_reduce_fusion
  226.0 9.5 %all-to-all-done = bf16[16,8,8]{1,2,0:T(8,128)(2,1)S(1)} async-done(((bf16[16,8,8]{1,2,0:T(8,128)(2,1)}), bf16[16,8,8]{1,2,0:T(8,128)(2,1)S(1)}, u32[]{:S(2)}, u32[]{:S(2)}) %all-to-all-start) | async-done | bytes 2080 | tf_op jit(solution)/shard_map/all_to_all | solution.py:74
  235.5 0.7 broadcast_multiply_fusion
  236.3 3.5 all-to-all-start.4
  239.8 0.4 fusion.3
  240.3 1.7 fusion
  242.0 9.4 %all-to-all-done.4 = f32[16,8,8]{1,2,0:T(8,128)S(1)} async-done(((f32[16,8,8]{1,2,0:T(8,128)}), f32[16,8,8]{1,2,0:T(8,128)S(1)}, u32[]{:S(2)}, u32[]{:S(2)}) %all-to-all-start.4) | async-done | bytes 4128 | tf_op jit(solution)/shard_map/all_to_all | solution.py:99
  251.4 3.7 all-to-all-start.3
  255.1 1.4 dynamic-slice
  256.6 0.6 gather_fusion.1
  257.2 78.4 %all-to-all-done.3 = f32[16,8,3584]{2,1,0:T(8,128)S(1)} async-done(((f32[16,8,3584]{2,1,0:T(8,128)}), f32[16,8,3584]{2,1,0:T(8,128)S(1)}, u32[]{:S(2)}, u32[]{:S(2)}) %all-to-all-start.3) | async-done | bytes 1835040 | tf_op jit(solution)/shard_map/all_to_all | solution.py:96
  335.6 1.8 gather_fusion
  337.4 1.3 broadcast_select_fusion
  338.7 252.0 %all-reduce.4 = (bf16[64,3584]{1,0:T(8,128)(2,1)S(1)}, f32[64,8]{1,0:T(8,128)S(1)}) all-reduce(f32[64,3584]{1,0:T(8,128)S(1)} %broadcast_select_fusion, f32[64,8]{1,0:T(8,128)S(1)} %broadcast_select_fusion.1), channel_id=2, replica_groups=mesh['node'=16,'local'=64] {'local'}, use_global_device_ids=true, to_apply=%region_4.5.clone | all-reduce | flops 229888 | bytes 1380352
  590.7 1.3 dynamic-slice_convert_fusion
  592.1 1.2 constant_dynamic-slice_fusion
  (24 shorter events, 0.9 us)
Async XLA Ops:
  0.6 205.2 %copy-start = (bf16[1,3584,128]{2,1,0:T(8,128)(2,1)S(1)}, bf16[1,3584,128]{2,1,0:T(8,128)(2,1)}, u32[]{:S(2)}) copy-start(bf16[1,3584,128]{2,1,0:T(8,128)(2,1)} %param.11) | copy-start | bytes 2752516
  97.6 11.5 %copy-start.2 = (bf16[1,3584]{1,0:T(2,128)(2,1)S(1)}, bf16[1,3584]{1,0:T(2,128)(2,1)}, u32[]{:S(2)}) copy-start(bf16[1,3584]{1,0:T(2,128)(2,1)} %param.8) | copy-start | bytes 21508
  98.9 60.7 %all-to-all-start.2 = ((bf16[16,8,3584]{2,1,0:T(8,128)(2,1)}), bf16[16,8,3584]{2,1,0:T(8,128)(2,1)S(1)}, u32[]{:S(2)}, u32[]{:S(2)}) async-start(bf16[16,8,3584]{2,1,0:T(8,128)(2,1)} %fusion.2), calls=%async_computation.2 | async-start | bytes 1835008 | tf_op jit(solution)/shard_map/all_to_all | solution.py:64
  158.3 13.3 %copy-start.3 = (bf16[1,8]{1,0:T(2,128)(2,1)S(1)}, bf16[1,8]{1,0:T(2,128)(2,1)}, u32[]{:S(2)}) copy-start(bf16[1,8]{1,0:T(2,128)(2,1)} %param.9) | copy-start | bytes 52
  159.6 46.7 %copy-start.1 = (bf16[1,3584,128]{2,1,0:T(8,128)(2,1)S(1)}, bf16[1,3584,128]{2,1,0:T(8,128)(2,1)}, u32[]{:S(2)}) copy-start(bf16[1,3584,128]{2,1,0:T(8,128)(2,1)} %param.12) | copy-start | bytes 2752516
  159.6 53.6 %all-to-all-start.1 = ((bf16[16,8,3584]{2,1,0:T(8,128)(2,1)}), bf16[16,8,3584]{2,1,0:T(8,128)(2,1)}, u32[]{:S(2)}, u32[]{:S(2)}) async-start(bf16[16,8,3584]{2,1,0:T(8,128)(2,1)} %fusion.1), calls=%async_computation.1 | async-start | bytes 1835008 | tf_op jit(solution)/shard_map/all_to_all | solution.py:67
  213.2 22.3 %all-to-all-start = ((bf16[16,8,8]{1,2,0:T(8,128)(2,1)}), bf16[16,8,8]{1,2,0:T(8,128)(2,1)S(1)}, u32[]{:S(2)}, u32[]{:S(2)}) async-start(bf16[16,8,8]{1,2,0:T(8,128)(2,1)} %copy.13), calls=%async_computation | async-start | bytes 65536 | tf_op jit(solution)/shard_map/all_to_all | solution.py:74
  236.3 15.1 %all-to-all-start.4 = ((f32[16,8,8]{1,2,0:T(8,128)}), f32[16,8,8]{1,2,0:T(8,128)S(1)}, u32[]{:S(2)}, u32[]{:S(2)}) async-start(f32[16,8,8]{1,2,0:T(8,128)} %get-tuple-element.6), calls=%async_computation.4 | async-start | bytes 131072 | tf_op jit(solution)/shard_map/all_to_all | solution.py:99
  251.4 84.2 %all-to-all-start.3 = ((f32[16,8,3584]{2,1,0:T(8,128)}), f32[16,8,3584]{2,1,0:T(8,128)S(1)}, u32[]{:S(2)}, u32[]{:S(2)}) async-start(f32[16,8,3584]{2,1,0:T(8,128)} %fusion), calls=%async_computation.3 | async-start | bytes 3670016 | tf_op jit(solution)/shard_map/all_to_all | solution.py:96
where the time goes:
time: 599 us; the launch traced here: 593 us
  blocking collectives  430 us (72%)
  waiting for transfers between devices  104 us (17%)
  starting transfers between devices  40.1 us (7%)
  matrix products  7.83 us (1%)
  local copies, waits for them, and re-layouts  7.33 us (1%)
    unnamed x1, blocking collectives  252 us
    all_to_all x1, waiting for transfers between devices, on_device(): lax.all_to_all(input_terms.reshape(leading, items, width), 'node', split_...  78.4 us
    all_gather x1, blocking collectives, on_device(): lax.all_gather(out_grad, 'local', axis=0, tiled=True)  49.2 us
    all_gather x1, blocking collectives, on_device(): lax.all_gather(tokens, 'local', axis=0, tiled=True)  48.7 us
    all_gather x1, blocking collectives, on_device(): lax.all_gather(dest_half, 'local', axis=0, tiled=True)  46.9 us
    all_gather x1, blocking collectives, on_device(): lax.all_gather(gate_prob, 'local', axis=0, tiled=True)  33.3 us
  transfers between devices with their start and end apart: 5, of which 4 were waited for; matrix products, arithmetic and copies ran while one was open for 2% of the time, Pallas kernels for 0%

commit v1 on v0

v1 whole, which is shorter than its diff:
```python
import jax
import jax.numpy as jnp
from jax import lax
from jax.experimental import pallas as pl
from jax.experimental.pallas import tpu as pltpu
from jax.sharding import Mesh
from jax.sharding import PartitionSpec as P

AXES = ("z", "yh", "yl", "x", "c")
LOCAL = ("yh", "yl", "x", "c")
QUAD = ("yl", "x")
F32 = jnp.float32
BF16 = jnp.bfloat16
LANES = 128
SLOTS = 8
NT = (((1,), (1,)), ((), ()))
TN = (((0,), (0,)), ((), ()))


def dot(a, b, dims=(((1,), (0,)), ((), ()))):
    return lax.dot_general(a, b, dims, preferred_element_type=F32)


def exchange(value, axes):
    return lax.all_to_all(value, axes, split_axis=0, concat_axis=0, tiled=True)


def place_kernel(where_ref, got_ref, send_ref, place_ref, wide):
    tokens, slots = place_ref.shape
    wide[...] = got_ref[...].astype(F32)
    aux = wide[pl.ds(4, tokens, stride=8), :]
    lane = lax.broadcasted_iota(jnp.int32, (tokens, LANES), 1)
    pair = where_ref[0]
    dest = jnp.sum(jnp.where(lane == 8 + 2 * pair, aux, 0.0), axis=1, keepdims=True)
    named = (dest == lane.astype(F32)).astype(F32)
    row = lax.broadcasted_iota(jnp.int32, (tokens, tokens), 0)
    col = lax.broadcasted_iota(jnp.int32, (tokens, tokens), 1)
    earlier = (col < row).astype(F32).astype(BF16)
    before = dot(earlier, named.astype(BF16))
    rank = jnp.sum(before * named, axis=1, keepdims=True)
    code = dest * SLOTS + rank
    slot = lax.broadcasted_iota(jnp.int32, (tokens, slots), 1).astype(F32)
    place = (code == slot).astype(F32).astype(BF16)
    place_ref[...] = place
    for k in range(4):
        part = wide[pl.ds(k, tokens, stride=8), :].astype(BF16)
        send_ref[:, k * LANES : (k + 1) * LANES] = dot(place, part, TN).astype(BF16)


def place_rows(where, got, slots):
    tokens = got.shape[0]
    return pl.pallas_call(
        place_kernel,
        out_shape=(
            jax.ShapeDtypeStruct((slots, 4 * LANES), BF16),
            jax.ShapeDtypeStruct((tokens, slots), BF16),
        ),
        in_specs=[
            pl.BlockSpec(memory_space=pltpu.SMEM),
            pl.BlockSpec(memory_space=pltpu.VMEM),
        ],
        out_specs=(
            pl.BlockSpec(memory_space=pltpu.VMEM),
            pl.BlockSpec(memory_space=pltpu.VMEM),
        ),
        scratch_shapes=[pltpu.VMEM((tokens * 8, LANES), F32)],
    )(where, got.reshape(tokens * 8, LANES))


def expert_kernel(where_ref, own_ref, oth_ref, wg_ref, wu_ref, wd_ref, keep_ref, give_ref):
    column, core = where_ref[1], where_ref[2]
    rows = own_ref.shape[1]
    gate = jnp.zeros((rows, LANES), F32)
    up = jnp.zeros((rows, LANES), F32)
    back = jnp.zeros((rows, LANES), F32)
    half = 3 * LANES

    def last_tile(q):
        mine = own_ref[q, :, half:]
        other = oth_ref[q, :, half:]
        return jnp.where(core == 0, mine, other), jnp.where(core == 0, other, mine)

    for i in range(4):
        base = 7 * LANES * i
        lo = pl.multiple_of(base + half * core, LANES)
        hi = pl.multiple_of(base + half * (1 - core), LANES)
        tail, _ = last_tile(i)
        for at, width, v in (
            (lo, half, own_ref[i, :, :half]),
            (hi, half, oth_ref[i, :, :half]),
            (base + 2 * half, LANES, tail),
        ):
            gate += dot(v, wg_ref[pl.ds(at, width), :])
            up += dot(v, wu_ref[pl.ds(at, width), :])
        tail, _ = last_tile(4 + i)
        for at, width, v in (
            (lo, half, own_ref[4 + i, :, :half]),
            (hi, half, oth_ref[4 + i, :, :half]),
            (base + 2 * half, LANES, tail),
        ):
            back += dot(v, wd_ref[:, pl.ds(at, width)], NT)

    _, aux = last_tile(0)
    lane = lax.broadcasted_iota(jnp.int32, (rows, LANES), 1)
    prob = jnp.sum(jnp.where(lane == column, aux.astype(F32), 0.0), axis=1, keepdims=True)
    logistic = jax.nn.sigmoid(gate)
    swished = gate * logistic
    gate_terms = jnp.sum(swished * up * back, axis=1, keepdims=True)
    scaled = prob * back
    grad_gate = (scaled * up * logistic * (1.0 + gate * (1.0 - logistic))).astype(BF16)
    grad_up = (scaled * swished).astype(BF16)
    width = keep_ref.shape[2]
    for ref, side in ((give_ref, 1 - core), (keep_ref, core)):
        for q in range(7):
            at = pl.ds(pl.multiple_of(2 * width * q + width * side, width), width)
            terms = dot(grad_gate, wg_ref[at, :], NT) + dot(grad_up, wu_ref[at, :], NT)
            ref[q] = terms.astype(ref.dtype)
        wide = lax.broadcasted_iota(jnp.int32, (rows, width), 1)
        here = jnp.logical_and(wide == column, side == 0)
        ref[7] = jnp.where(here, gate_terms, 0.0).astype(ref.dtype)


def expert_terms(where, own, oth, wg, wu, wd):
    rows = own.shape[1]
    return pl.pallas_call(
        expert_kernel,
        out_shape=(
            jax.ShapeDtypeStruct((8, rows, 2 * LANES), F32),
            jax.ShapeDtypeStruct((8, rows, 2 * LANES), BF16),
        ),
        in_specs=[pl.BlockSpec(memory_space=pltpu.SMEM)]
        + [pl.BlockSpec(memory_space=pltpu.VMEM)] * 5,
        out_specs=(
            pl.BlockSpec(memory_space=pltpu.VMEM),
            pl.BlockSpec(memory_space=pltpu.VMEM),
        ),
        compiler_params=pltpu.CompilerParams(vmem_limit_bytes=32 * 1024 * 1024),
        cost_estimate=pl.CostEstimate(
            flops=10 * rows * 3584 * LANES, bytes_accessed=6 << 20, transcendentals=rows * LANES
        ),
    )(where, own, oth, wg, wu, wd)


def on_device(tokens, out_grad, gate_prob, dest_node, w_gate, w_up, w_down):
    nodes = lax.axis_size("z")
    width = tokens.shape[1]
    slots = nodes * SLOTS
    pair = lax.axis_index("yh")
    core = lax.axis_index("c")
    where = jnp.stack([pair, 2 * pair + lax.axis_index("yl"), core]).astype(jnp.int32)

    pieces = jnp.concatenate(
        [tokens.reshape(4, 7, LANES), out_grad.reshape(4, 7, LANES)], axis=0
    )
    aux = jnp.concatenate([gate_prob[0], dest_node[0].astype(BF16)])
    aux = jnp.broadcast_to(jnp.pad(aux, (0, LANES - 16)), (8, 1, LANES))
    first = jnp.concatenate([pieces[:, :3], pieces[:, 6:7], aux], axis=1)
    second = jnp.concatenate([pieces[:, 3:6], aux, aux], axis=1)
    both = jnp.pad(jnp.stack([first, second], axis=1), ((0, 0), (0, 0), (0, 3), (0, 0)))
    out = jnp.broadcast_to(both.reshape(1, 16, 8, LANES), (4, 16, 8, LANES))
    got = exchange(out.reshape(64, 8, LANES), LOCAL)

    send, place = place_rows(where, got, 16 * SLOTS)
    send = send[:slots]
    rows = exchange(send.reshape(nodes, SLOTS, 4 * LANES), "z").reshape(slots, 4 * LANES)

    own = exchange(jnp.broadcast_to(rows[None], (8, slots, 4 * LANES)), QUAD)
    swap = ((0, 1), (1, 0))
    oth = lax.ppermute(own, "c", swap)
    keep, give = expert_terms(where, own, oth, w_gate[0], w_up[0], w_down[0])

    took = lax.ppermute(give, "c", swap)
    terms = exchange((keep + took.astype(F32)).astype(BF16), QUAD)
    summed = jnp.sum(terms.astype(F32), axis=0).astype(BF16)

    back = exchange(summed.reshape(nodes, SLOTS, 2 * LANES), "z").reshape(slots, 2 * LANES)
    chosen = dot(place[:, :slots], back).astype(BF16)
    home = exchange(chosen.reshape(64, 2, LANES), LOCAL)
    total = jnp.sum(home.reshape(4, 16, 2 * LANES).astype(F32), axis=0)
    in_grad = total[: width // (2 * LANES)].reshape(1, width).astype(BF16)
    return in_grad, total[14:15, :8]


def solution(mesh):
    fine = Mesh(mesh.devices.reshape(mesh.devices.shape[0], 4, 2, 4, 2), AXES)
    row = P(AXES, None)
    block = P(AXES, None, None)
    return jax.shard_map(
        on_device,
        mesh=fine,
        in_specs=(row, row, row, row, block, block, block),
        out_specs=(row, row),
        check_vma=False,
    )
```

time: 599 us -> 138 us (0.23)
  blocking collectives: 430 us -> 83.5 us
  waiting for transfers between devices: 104 us -> 14.5 us
  starting transfers between devices: 40.1 us -> 27.5 us
  matrix products: 7.83 us -> 0.13 us
    unnamed x1 -> x0, blocking collectives: 252 us -> none
    all_gather x4 -> x0, blocking collectives: 178 us -> none  [the longest x1 49.2 us: on_device(): lax.all_gather(out_grad, 'local', axis=0, tiled=True)]
    all_to_all x5 -> x1, waiting for transfers between devices: 104 us -> 10.7 us  [exchange(): return lax.all_to_all(value, axes, split_axis=0, concat_axis=0, tiled=True)]
    all_to_all x0 -> x5, blocking collectives: none -> 83.5 us  [exchange(): return lax.all_to_all(value, axes, split_axis=0, concat_axis=0, tiled=True)]
    all_to_all x5 -> x1, starting transfers between devices: 40.1 us -> 18.2 us  [exchange(): return lax.all_to_all(value, axes, split_axis=0, concat_axis=0, tiled=True)]
    ppermute x0 -> x2, starting transfers between devices: none -> 9.3 us  [the longest x1 7.02 us: on_device(): oth = lax.ppermute(own, 'c', swap)]
    dot_general x8 -> x1, matrix products: 7.83 us -> 0.13 us  [dot(): return lax.dot_general(a, b, dims, preferred_element_type=F32)]
  transfers between devices with their start and end apart: 5 -> 3, of which waited for: 4 -> 3; matrix products, arithmetic and copies ran while one was open for 2% -> 0% of each run, Pallas kernels for 0% -> 0%
where the time goes in v1:
time: 138 us
  blocking collectives  83.5 us (61%)
  starting transfers between devices  27.5 us (20%)
  waiting for transfers between devices  14.5 us (11%)
  local copies, waits for them, and re-layouts  5.26 us (4%)
  Pallas kernels  4.32 us (3%)
  other arithmetic  1.78 us (1%)
    all_to_all x5, blocking collectives, exchange(): return lax.all_to_all(value, axes, split_axis=0, concat_axis=0, tiled=True)  83.5 us
    all_to_all x1, starting transfers between devices, exchange(): return lax.all_to_all(value, axes, split_axis=0, concat_axis=0, tiled=True)  18.2 us
    all_to_all x1, waiting for transfers between devices, exchange(): return lax.all_to_all(value, axes, split_axis=0, concat_axis=0, tiled=True)  10.7 us
    ppermute x1, starting transfers between devices, on_device(): oth = lax.ppermute(own, 'c', swap)  7.02 us
    unnamed x22, local copies, waits for them, and re-layouts  3.88 us
  transfers between devices with their start and end apart: 3, of which 3 were waited for; matrix products, arithmetic and copies ran while one was open for 0% of the time, Pallas kernels for 0%

profile of v1, /device:TPU:1, one launch (start us, length us, event | category | flops | bytes accessed | tf_op | source)
XLA Modules:
  0.0 137.8 jit_solution(10406770826054045474)
XLA Ops:
  0.6 0.8 reduce.1
  1.4 0.7 copy-done.6
  2.1 0.1 reduce.2
  2.2 0.0 copy-start.7
  2.2 0.6 copy-done.7
  2.9 0.7 copy-done.8
  3.5 0.1 fusion.4
  3.7 0.7 broadcast_in_dim.19
  4.4 18.2 %all-to-all-start = ((bf16[64,8,128]{2,1,0:T(8,128)(2,1)}), bf16[64,8,128]{2,1,0:T(8,128)(2,1)S(1)}, u32[]{:S(2)}, u32[]{:S(2)}) async-start(bf16[64,8,128]{2,1,0:T(8,128)(2,1)} %bitcast.8), calls=%async_computation | async-start | bytes 262144 | tf_op jit(solution)/shard_map/all_to_all | solution.py:25
  22.6 0.6 pad_add_fusion.where_ref
  23.2 10.7 %all-to-all-done = bf16[64,8,128]{2,1,0:T(8,128)(2,1)S(1)} async-done(((bf16[64,8,128]{2,1,0:T(8,128)(2,1)}), bf16[64,8,128]{2,1,0:T(8,128)(2,1)S(1)}, u32[]{:S(2)}, u32[]{:S(2)}) %all-to-all-start) | async-done | bytes 131104 | tf_op jit(solution)/shard_map/all_to_all | solution.py:25
  33.9 0.6 copy-done.4
  34.6 2.1 %shard_map.86 = (bf16[128,512]{1,0:T(8,128)(2,1)}, bf16[64,128]{1,0:T(8,128)(2,1)}) custom-call(s32[3]{0:T(128)} %pad_add_fusion.where_ref, bf16[512,128]{1,0:T(8,128)(2,1)} %bitcast.31), custom_call_target="tpu_custom_call" | custom-call | tf_op jit(solution)/shard_map/pallas_call | solution.py:52
  36.6 23.9 %all_to_all.30 = bf16[16,8,512]{2,1,0:T(8,128)(2,1)S(1)} all-to-all(bf16[16,8,512]{2,1,0:T(8,128)(2,1)} %bitcast.34), channel_id=1, replica_groups=mesh['z'=16,'yh'=4,'yl'=2,'x'=4,'c'=2] {'z'}, dimensions={0} | all-to-all | bytes 262144 | tf_op jit(solution)/shard_map/all_to_all | solution.py:25
  60.5 0.1 broadcast_in_dim.21
  60.6 0.0 copy-start
  60.7 0.0 copy-start.1
  60.7 14.1 %all_to_all.31.own_ref = bf16[8,128,512]{2,1,0:T(8,128)(2,1)S(1)} all-to-all(bf16[8,128,512]{2,1,0:T(8,128)(2,1)S(1)} %broadcast_in_dim.21), channel_id=1, replica_groups=mesh['z'=16,'yh'=4,'yl'=2,'x'=4,'c'=2] {'yl','x'}, dimensions={0} | all-to-all | bytes 2097152 | tf_op jit(solution)/shard_map/all_to_all | solution.py:25
  74.8 7.0 %collective-permute-start = (bf16[8,128,512]{2,1,0:T(8,128)(2,1)S(1)}, bf16[8,128,512]{2,1,0:T(8,128)(2,1)S(1)}, u32[]{:S(2)}, u32[]{:S(2)}) collective-permute-start(bf16[8,128,512]{2,1,0:T(8,128)(2,1)S(1)} %all_to_all.31.own_ref), channel_id=1, source_target_pairs={{0,1},{1,0},{2,3},{3,2},{4,5},{5,4},{6,7},{7,6},{8,9},{9,8},{10,11... | collective-permute-start | bytes 3145736 | tf_op jit(solution)/shard_map/ppermute | solution.py:169
  81.8 2.3 %collective-permute-done.oth_ref = bf16[8,128,512]{2,1,0:T(8,128)(2,1)S(1)} collective-permute-done((bf16[8,128,512]{2,1,0:T(8,128)(2,1)S(1)}, bf16[8,128,512]{2,1,0:T(8,128)(2,1)S(1)}, u32[]{:S(2)}, u32[]{:S(2)}) %collective-permute-start) | collective-permute-done | bytes 1048608 | tf_op jit(solution)/shard_map/ppermute | solution.py:169
  84.1 0.6 copy-done.3
  84.7 2.2 %shard_map.87 = (f32[8,128,256]{2,1,0:T(8,128)S(1)}, bf16[8,128,256]{2,1,0:T(8,128)(2,1)S(1)}) custom-call(s32[3]{0:T(128)S(1)} %copy-done.3, bf16[8,128,512]{2,1,0:T(8,128)(2,1)S(1)} %all_to_all.31.own_ref, bf16[8,128,512]{2,1,0:T(8,128)(2,1)S(1)} %collective-permute-done.oth_ref, bf16[3584,128]{1,0:T(8,128)(2,1)S(1)} %bitcast.27, ...), custom_call_target="tpu_custom_call" | custom-call | flops 587202560 | bytes 6291456 | tf_op jit(solution)/shard_map/pallas_call | solution.py:125
  87.0 2.3 %collective-permute-start.1 = (bf16[8,128,256]{2,1,0:T(8,128)(2,1)S(1)}, bf16[8,128,256]{2,1,0:T(8,128)(2,1)S(1)}, u32[]{:S(2)}, u32[]{:S(2)}) collective-permute-start(bf16[8,128,256]{2,1,0:T(8,128)(2,1)S(1)} %get-tuple-element.9), channel_id=1, source_target_pairs={{0,1},{1,0},{2,3},{3,2},{4,5},{5,4},{6,7},{7,6},{8,9},{9,8},{10,11... | collective-permute-start | bytes 1572872 | tf_op jit(solution)/shard_map/ppermute | solution.py:172
  89.3 1.5 %collective-permute-done.1 = bf16[8,128,256]{2,1,0:T(8,128)(2,1)S(1)} collective-permute-done((bf16[8,128,256]{2,1,0:T(8,128)(2,1)S(1)}, bf16[8,128,256]{2,1,0:T(8,128)(2,1)S(1)}, u32[]{:S(2)}, u32[]{:S(2)}) %collective-permute-start.1) | collective-permute-done | bytes 524320 | tf_op jit(solution)/shard_map/ppermute | solution.py:172
  90.8 0.1 add_convert_fusion
  90.9 11.1 %all_to_all.32 = bf16[8,128,256]{2,1,0:T(8,128)(2,1)S(1)} all-to-all(bf16[8,128,256]{2,1,0:T(8,128)(2,1)S(1)} %add_convert_fusion), channel_id=1, replica_groups=mesh['z'=16,'yh'=4,'yl'=2,'x'=4,'c'=2] {'yl','x'}, dimensions={0} | all-to-all | bytes 1048576 | tf_op jit(solution)/shard_map/all_to_all | solution.py:25
  102.0 0.1 reduce_sum.21
  102.1 18.1 %all_to_all.33 = bf16[16,8,256]{2,1,0:T(8,128)(2,1)S(1)} all-to-all(bf16[16,8,256]{2,1,0:T(8,128)(2,1)S(1)} %bitcast.32), channel_id=1, replica_groups=mesh['z'=16,'yh'=4,'yl'=2,'x'=4,'c'=2] {'z'}, dimensions={0} | all-to-all | bytes 131072 | tf_op jit(solution)/shard_map/all_to_all | solution.py:25
  120.2 0.1 convolution_convert_fusion
  120.4 16.3 %all_to_all.34 = bf16[64,2,128]{2,1,0:T(2,128)(2,1)S(1)} all-to-all(bf16[64,2,128]{2,1,0:T(2,128)(2,1)S(1)} %reshape.56), channel_id=1, replica_groups=mesh['z'=16,'yh'=4,'yl'=2,'x'=4,'c'=2] {'yh','yl','x','c'}, dimensions={0} | all-to-all | bytes 65536 | tf_op jit(solution)/shard_map/all_to_all | solution.py:25
  136.7 0.5 slice.25
  137.2 0.6 copy.11
  (26 shorter events, 0.2 us)
Async XLA Ops:
  1.4 0.7 copy-start.6
  2.2 0.7 copy-start.7
  2.9 0.7 copy-start.8
  4.4 29.6 %all-to-all-start = ((bf16[64,8,128]{2,1,0:T(8,128)(2,1)}), bf16[64,8,128]{2,1,0:T(8,128)(2,1)S(1)}, u32[]{:S(2)}, u32[]{:S(2)}) async-start(bf16[64,8,128]{2,1,0:T(8,128)(2,1)} %bitcast.8), calls=%async_computation | async-start | bytes 262144 | tf_op jit(solution)/shard_map/all_to_all | solution.py:25
  33.9 0.6 copy-start.4
  60.5 23.6 %copy-start.2 = (bf16[1,128,3584]{2,1,0:T(8,128)(2,1)S(1)}, bf16[1,128,3584]{2,1,0:T(8,128)(2,1)}, u32[]{:S(2)}) copy-start(bf16[1,128,3584]{2,1,0:T(8,128)(2,1)} %param.13) | copy-start | bytes 2752516
  60.6 23.5 %copy-start = (bf16[1,3584,128]{2,1,0:T(8,128)(2,1)S(1)}, bf16[1,3584,128]{2,1,0:T(8,128)(2,1)}, u32[]{:S(2)}) copy-start(bf16[1,3584,128]{2,1,0:T(8,128)(2,1)} %param.11) | copy-start | bytes 2752516
  60.7 23.5 %copy-start.1 = (bf16[1,3584,128]{2,1,0:T(8,128)(2,1)S(1)}, bf16[1,3584,128]{2,1,0:T(8,128)(2,1)}, u32[]{:S(2)}) copy-start(bf16[1,3584,128]{2,1,0:T(8,128)(2,1)} %param.12) | copy-start | bytes 2752516
  74.8 9.3 %collective-permute-start = (bf16[8,128,512]{2,1,0:T(8,128)(2,1)S(1)}, bf16[8,128,512]{2,1,0:T(8,128)(2,1)S(1)}, u32[]{:S(2)}, u32[]{:S(2)}) collective-permute-start(bf16[8,128,512]{2,1,0:T(8,128)(2,1)S(1)} %all_to_all.31.own_ref), channel_id=1, source_target_pairs={{0,1},{1,0},{2,3},{3,2},{4,5},{5,4},{6,7},{7,6},{8,9},{9,8},{10,11... | collective-permute-start | bytes 3145736 | tf_op jit(solution)/shard_map/ppermute | solution.py:169
  84.1 0.6 copy-start.3
  87.0 3.8 %collective-permute-start.1 = (bf16[8,128,256]{2,1,0:T(8,128)(2,1)S(1)}, bf16[8,128,256]{2,1,0:T(8,128)(2,1)S(1)}, u32[]{:S(2)}, u32[]{:S(2)}) collective-permute-start(bf16[8,128,256]{2,1,0:T(8,128)(2,1)S(1)} %get-tuple-element.9), channel_id=1, source_target_pairs={{0,1},{1,0},{2,3},{3,2},{4,5},{5,4},{6,7},{7,6},{8,9},{9,8},{10,11... | collective-permute-start | bytes 1572872 | tf_op jit(solution)/shard_map/ppermute | solution.py:172
  102.1 18.1 %copy-start.5 = (bf16[64,128]{1,0:T(8,128)(2,1)S(1)}, bf16[64,128]{1,0:T(8,128)(2,1)}, u32[]{:S(2)}) copy-start(bf16[64,128]{1,0:T(8,128)(2,1)} %get-tuple-element.6) | copy-start | bytes 49156

commit v2 on v1

v2 whole, which is shorter than its diff:
```python
import jax
import jax.numpy as jnp
from jax import lax
from jax.experimental import pallas as pl
from jax.experimental.pallas import tpu as pltpu
from jax.sharding import Mesh
from jax.sharding import PartitionSpec as P

AXES = ("z", "yh", "yl", "x", "c")
LOCAL = ("yh", "yl", "x", "c")
QUAD = ("yl", "x")
SWAP = ((0, 1), (1, 0))
F32 = jnp.float32
BF16 = jnp.bfloat16
LANES = 128
TILES = 7
PIECE = TILES * LANES
HALF = 4
BACK = 512
NT = (((1,), (1,)), ((), ()))
TN = (((0,), (0,)), ((), ()))
VMEM = pl.BlockSpec(memory_space=pltpu.VMEM)
HBM = pl.BlockSpec(memory_space=pltpu.HBM)
WHOLE = 56
MOST = 51
MIB = 1024 * 1024


def dot(a, b, dims=(((1,), (0,)), ((), ()))):
    return lax.dot_general(a, b, dims, preferred_element_type=F32)


def exchange(value, axes):
    return lax.all_to_all(value, axes, split_axis=0, concat_axis=0, tiled=True)


def pack_kernel(x_hbm, dy_hbm, gate_hbm, dest_hbm, out_ref, x_ref, dy_ref, gate_ref, dest_ref, arrived):
    copies = [
        pltpu.make_async_copy(source, target, arrived.at[i])
        for i, (source, target) in enumerate(
            ((x_hbm, x_ref), (dy_hbm, dy_ref), (gate_hbm, gate_ref), (dest_hbm, dest_ref))
        )
    ]
    for copy in copies:
        copy.start()
    for copy in copies:
        copy.wait()
    gate = gate_ref[...].astype(F32)
    dest = dest_ref[...].astype(F32)
    aux = jnp.concatenate([gate, dest, jnp.zeros((1, LANES - 16), F32)], axis=1)
    for q in range(8):
        ref, base = (x_ref, q * PIECE) if q < 4 else (dy_ref, (q - 4) * PIECE)
        rows = [ref[:, base + k * LANES : base + (k + 1) * LANES].astype(F32) for k in range(TILES)]
        tile = jnp.concatenate(rows + [aux], axis=0).astype(BF16)
        for pair in range(4):
            for core in range(2):
                out_ref[pair * 16 + q * 2 + core] = tile


def place_kernel(got_ref, send_ref, place_ref, wide):
    tokens, slots = place_ref.shape
    pair = lax.axis_index("yh")
    core = lax.axis_index("c")
    wide[...] = got_ref[...].astype(F32)
    aux = wide[pl.ds(TILES, tokens, stride=8), :]
    lane = lax.broadcasted_iota(jnp.int32, (tokens, LANES), 1)
    dest = jnp.sum(jnp.where(lane == 8 + 2 * pair, aux, 0.0), axis=1, keepdims=True)
    named = (dest == lane.astype(F32)).astype(F32)
    row = lax.broadcasted_iota(jnp.int32, (tokens, tokens), 0)
    col = lax.broadcasted_iota(jnp.int32, (tokens, tokens), 1)
    earlier = (col < row).astype(F32).astype(BF16)
    before = dot(earlier, named.astype(BF16))
    rank = jnp.sum(before * named, axis=1, keepdims=True)
    slot = lax.broadcasted_iota(jnp.int32, (tokens, slots), 1).astype(F32)
    at = rank - HALF * core.astype(F32)
    code = jnp.where(jnp.logical_and(at >= 0.0, at < HALF), dest * HALF + at, -1.0)
    place = (code == slot).astype(F32).astype(BF16)
    place_ref[...] = place
    for k in range(TILES + 1):
        part = wide[pl.ds(k, tokens, stride=8), :].astype(BF16)
        send_ref[:, k * LANES : (k + 1) * LANES] = dot(place, part, TN).astype(BF16)


def expert_kernel(aux_ref, rows_ref, *refs):
    sources, (out_ref, *weights, arrived) = refs[:6], refs[6:]
    copies = [
        pltpu.make_async_copy(source, target, arrived.at[i])
        for i, (source, target) in enumerate(zip(sources, weights))
    ]
    for copy in copies:
        copy.start()
    column = 2 * lax.axis_index("yh") + lax.axis_index("yl")
    rows = rows_ref.shape[1]
    lane = lax.broadcasted_iota(jnp.int32, (rows, LANES), 1)
    prob = jnp.where(lane == column, aux_ref[...].astype(F32), 0.0)
    prob = jnp.sum(prob, axis=1, keepdims=True)
    gate_terms = jnp.zeros((rows, 1), F32)
    grads = []
    for core in range(2):
        gate_w, up_w, down_w = weights[3 * core : 3 * core + 3]
        for copy in copies[3 * core : 3 * core + 3]:
            copy.wait()
        gate = jnp.zeros((rows, LANES), F32)
        up = jnp.zeros((rows, LANES), F32)
        back = jnp.zeros((rows, LANES), F32)
        for i in range(4):
            at = slice(i * PIECE, (i + 1) * PIECE)
            gate += dot(rows_ref[i], gate_w[at, :])
            up += dot(rows_ref[i], up_w[at, :])
            back += dot(rows_ref[4 + i], down_w[:, at], NT)
        logistic = jax.nn.sigmoid(gate)
        swished = gate * logistic
        gate_terms += jnp.sum(swished * up * back, axis=1, keepdims=True)
        scaled = prob * back
        slope = scaled * up * logistic * (1.0 + gate * (1.0 - logistic))
        grads += [(slope.astype(BF16), gate_w), ((scaled * swished).astype(BF16), up_w)]
    for q in range(7):
        at = slice(q * BACK, (q + 1) * BACK)
        terms = sum(dot(grad, weight[at, :], NT) for grad, weight in grads)
        out_ref[q] = terms.astype(BF16)
    wide = lax.broadcasted_iota(jnp.int32, (rows, BACK), 1)
    out_ref[7] = jnp.where(wide == column, gate_terms, 0.0).astype(BF16)


def on_device(tokens, out_grad, gate_prob, dest_node, w_gate, w_up, w_down):
    nodes = lax.axis_size("z")
    width = tokens.shape[1]
    slots = nodes * HALF
    weights = (w_gate[0], w_up[0], w_down[0])

    out = pl.pallas_call(
        pack_kernel,
        out_shape=jax.ShapeDtypeStruct((64, 8, LANES), BF16),
        in_specs=[HBM] * 4,
        out_specs=VMEM,
        scratch_shapes=[
            pltpu.VMEM(tokens.shape, BF16),
            pltpu.VMEM(out_grad.shape, BF16),
            pltpu.VMEM(gate_prob.shape, BF16),
            pltpu.VMEM(dest_node.shape, jnp.int32),
            pltpu.SemaphoreType.DMA((4,)),
        ],
        compiler_params=pltpu.CompilerParams(vmem_limit_bytes=WHOLE * MIB),
    )(tokens, out_grad, gate_prob, dest_node)
    got = exchange(out, LOCAL)

    send, place = pl.pallas_call(
        place_kernel,
        out_shape=(
            jax.ShapeDtypeStruct((16 * HALF, PIECE + LANES), BF16),
            jax.ShapeDtypeStruct((64, 16 * HALF), BF16),
        ),
        in_specs=[VMEM],
        out_specs=(VMEM, VMEM),
        scratch_shapes=[pltpu.VMEM((64 * 8, LANES), F32)],
        compiler_params=pltpu.CompilerParams(vmem_limit_bytes=4 * MIB),
    )(got.reshape(64 * 8, LANES))
    rows = exchange(send[:slots].reshape(nodes, HALF, PIECE + LANES), "z")
    rows = rows.reshape(slots, PIECE + LANES)

    others = [lax.ppermute(weight, "c", SWAP) for weight in weights]
    own = exchange(jnp.broadcast_to(rows[None, :, :PIECE], (8, slots, PIECE)), QUAD)
    partial = pl.pallas_call(
        expert_kernel,
        out_shape=jax.ShapeDtypeStruct((8, slots, BACK), BF16),
        in_specs=[VMEM] * 2 + [HBM] * 6,
        out_specs=VMEM,
        scratch_shapes=[
            *[pltpu.VMEM(weight.shape, BF16) for weight in (*weights, *weights)],
            pltpu.SemaphoreType.DMA((6,)),
        ],
        compiler_params=pltpu.CompilerParams(vmem_limit_bytes=MOST * MIB),
        cost_estimate=pl.CostEstimate(
            flops=20 * slots * width * LANES,
            bytes_accessed=8 * MIB,
            transcendentals=2 * slots * LANES,
        ),
    )(rows[:, PIECE:], own, *weights, *others)

    terms = exchange(partial, QUAD)
    summed = jnp.sum(terms.astype(F32), axis=0).astype(BF16)

    back = exchange(summed.reshape(nodes, HALF, BACK), "z").reshape(slots, BACK)
    chosen = dot(place[:, :slots], back).astype(BF16)
    home = exchange(chosen.reshape(64, BACK // LANES, LANES), LOCAL)
    total = jnp.sum(home.reshape(4, 8, 2, BACK).astype(F32), axis=(0, 2))
    return total[:7].reshape(1, width).astype(BF16), total[7:, :8]


def solution(mesh):
    fine = Mesh(mesh.devices.reshape(mesh.devices.shape[0], 4, 2, 4, 2), AXES)
    row = P(AXES, None)
    block = P(AXES, None, None)
    return jax.shard_map(
        on_device,
        mesh=fine,
        in_specs=(row, row, row, row, block, block, block),
        out_specs=(row, row),
        check_vma=False,
    )
```

time: 138 us -> 129 us (0.935)
  blocking collectives: 83.5 us -> 102 us
  starting transfers between devices: 27.5 us -> 13.2 us
  waiting for transfers between devices: 14.5 us -> 0.5 us
  Pallas kernels: 4.32 us -> 6.87 us
  other arithmetic: 1.78 us -> 0.14 us
    all_to_all x5, blocking collectives: 83.5 us -> 102 us  [exchange(): return lax.all_to_all(value, axes, split_axis=0, concat_axis=0, tiled=True)]
    all_to_all x1, starting transfers between devices: 18.2 us -> 3.68 us  [exchange(): return lax.all_to_all(value, axes, split_axis=0, concat_axis=0, tiled=True)]
    all_to_all x1, waiting for transfers between devices: 10.7 us -> 0.01 us  [exchange(): return lax.all_to_all(value, axes, split_axis=0, concat_axis=0, tiled=True)]
    ppermute x2 -> x3, waiting for transfers between devices: 3.78 us -> 0.49 us  [on_device(): others = [lax.ppermute(weight, 'c', SWAP) for weight in weights]]
    pallas_call x2 -> x3, Pallas kernels: 4.32 us -> 6.87 us  [the longest x1 4.85 us: on_device(): pl.pallas_call(expert_kernel, out_shape=jax.ShapeDtypeStruct((8, slots, B...]
    unnamed x22 -> x10, local copies, waits for them, and re-layouts: 3.88 us -> 2.51 us
    ppermute x2 -> x3, starting transfers between devices: 9.3 us -> 9.47 us  [on_device(): others = [lax.ppermute(weight, 'c', SWAP) for weight in weights]]
  transfers between devices with their start and end apart: 3 -> 4, of which waited for: 3 -> 1; matrix products, arithmetic and copies ran while one was open for 0% -> 0% of each run, Pallas kernels for 0% -> 0%
where the time goes in v2:
time: 129 us; the launch traced here: 128 us
  blocking collectives  102 us (79%)
  starting transfers between devices  13.2 us (10%)
  Pallas kernels  6.87 us (5%)
  local copies, waits for them, and re-layouts  4.32 us (3%)
    all_to_all x5, blocking collectives, exchange(): return lax.all_to_all(value, axes, split_axis=0, concat_axis=0, tiled=True)  102 us
    ppermute x3, starting transfers between devices, on_device(): others = [lax.ppermute(weight, 'c', SWAP) for weight in weights]  9.47 us
    pallas_call x1, Pallas kernels, on_device(): pl.pallas_call(expert_kernel, out_shape=jax.ShapeDtypeStruct((8, slots, B...  4.85 us
    all_to_all x1, starting transfers between devices, exchange(): return lax.all_to_all(value, axes, split_axis=0, concat_axis=0, tiled=True)  3.68 us
  transfers between devices with their start and end apart: 4, of which 1 were waited for; matrix products, arithmetic and copies ran while one was open for 0% of the time, Pallas kernels for 0%

profile of v2, /device:TPU:1, one launch (start us, length us, event | category | flops | bytes accessed | tf_op | source)
XLA Modules:
  0.0 128.0 jit_solution(16370080090721065394)
XLA Ops:
  0.6 1.5 %shard_map.86 = bf16[64,8,128]{2,1,0:T(8,128)(2,1)} custom-call(bf16[1,3584]{1,0:T(2,128)(2,1)} %x_hbm.1, bf16[1,3584]{1,0:T(2,128)(2,1)} %dy_hbm.1, bf16[1,8]{1,0:T(2,128)(2,1)} %gate_hbm.1, s32[1,8]{1,0:T(1,128)} %dest_hbm.1), custom_call_target="tpu_custom_call" | custom-call | tf_op jit(solution)/shard_map/pallas_call | solution.py:131
  2.1 29.6 %all_to_all.30 = bf16[64,8,128]{2,1,0:T(8,128)(2,1)S(1)} all-to-all(bf16[64,8,128]{2,1,0:T(8,128)(2,1)} %shard_map.86), channel_id=1, replica_groups=mesh['z'=16,'yh'=4,'yl'=2,'x'=4,'c'=2] {'yh','yl','x','c'}, dimensions={0} | all-to-all | bytes 262144 | tf_op jit(solution)/shard_map/all_to_all | solution.py:34
  31.7 0.5 shard_map.87
  32.3 0.1 reshape.41
  32.3 23.7 %all_to_all.31 = bf16[16,4,1024]{2,1,0:T(4,128)(2,1)S(1)} all-to-all(bf16[16,4,1024]{2,1,0:T(4,128)(2,1)S(1)} %reshape.41), channel_id=1, replica_groups=mesh['z'=16,'yh'=4,'yl'=2,'x'=4,'c'=2] {'z'}, dimensions={0} | all-to-all | bytes 262144 | tf_op jit(solution)/shard_map/all_to_all | solution.py:34
  56.1 1.0 broadcast_in_dim.2
  57.1 0.0 copy-start
  57.1 0.0 copy-start.1
  57.1 3.7 %all-to-all-start.2 = ((bf16[8,64,896]{2,1,0:T(8,128)(2,1)}), bf16[8,64,896]{2,1,0:T(8,128)(2,1)S(1)}, u32[]{:S(2)}, u32[]{:S(2)}) async-start(bf16[8,64,896]{2,1,0:T(8,128)(2,1)} %broadcast_in_dim.2), calls=%async_computation.2 | async-start | bytes 1835008 | tf_op jit(solution)/shard_map/all_to_all | solution.py:34
  60.8 0.0 copy-done
  60.8 5.1 %collective-permute-start = (bf16[3584,128]{1,0:T(8,128)(2,1)S(1)}, bf16[3584,128]{1,0:T(8,128)(2,1)S(1)}, u32[]{:S(2)}, u32[]{:S(2)}) collective-permute-start(bf16[3584,128]{1,0:T(8,128)(2,1)S(1)} %bitcast.10), channel_id=1, source_target_pairs={{0,1},{1,0},{2,3},{3,2},{4,5},{5,4},{6,7},{7,6},{8,9},{9,8},{10,11... | collective-permute-start | bytes 2752520 | tf_op jit(solution)/shard_map/ppermute | solution.py:161
  66.0 0.0 copy-done.1
  66.0 1.9 %collective-permute-start.1 = (bf16[3584,128]{1,0:T(8,128)(2,1)S(1)}, bf16[3584,128]{1,0:T(8,128)(2,1)S(1)}, u32[]{:S(2)}, u32[]{:S(2)}) collective-permute-start(bf16[3584,128]{1,0:T(8,128)(2,1)S(1)} %bitcast.14), channel_id=1, source_target_pairs={{0,1},{1,0},{2,3},{3,2},{4,5},{5,4},{6,7},{7,6},{8,9},{9,8},{10,11... | collective-permute-start | bytes 2752520 | tf_op jit(solution)/shard_map/ppermute | solution.py:161
  67.9 2.4 %collective-permute-start.2 = (bf16[128,3584]{1,0:T(8,128)(2,1)}, bf16[128,3584]{1,0:T(8,128)(2,1)}, u32[]{:S(2)}, u32[]{:S(2)}) collective-permute-start(bf16[128,3584]{1,0:T(8,128)(2,1)} %bitcast.15), channel_id=1, source_target_pairs={{0,1},{1,0},{2,3},{3,2},{4,5},{5,4},{6,7},{7,6},{8,9},{9,8},{10,11... | collective-permute-start | bytes 2752520 | tf_op jit(solution)/shard_map/ppermute | solution.py:161
  70.3 0.0 collective-permute-done.refs_3_
  70.3 0.0 copy-start.2
  70.3 0.0 collective-permute-done.1.refs_4_
  70.4 0.9 copy-done.2
  71.3 0.0 copy-start.3
  71.3 0.9 copy-done.3
  72.2 0.5 collective-permute-done.2.refs_5_
  72.7 0.0 all-to-all-done.2.rows_ref
  72.7 4.8 %shard_map.88 = bf16[8,64,512]{2,1,0:T(8,128)(2,1)S(1)} custom-call(bf16[64,128]{1,0:T(8,128)(2,1)S(1)} %slice.17.aux_ref, bf16[8,64,896]{2,1,0:T(8,128)(2,1)S(1)} %all-to-all-done.2.rows_ref, bf16[3584,128]{1,0:T(8,128)(2,1)S(1)} %bitcast.11, bf16[3584,128]{1,0:T(8,128)(2,1)} %bitcast.13, bf16[128,3584]{1,0:T(8,128)(2,1)} %bitcast.16, ...), custom_call_target="tpu_custom_call" | custom-call | flops 587202560 | bytes 8388608 | tf_op jit(solution)/shard_map/pallas_call | solution.py:163
  77.6 13.9 %all_to_all.32 = bf16[8,64,512]{2,1,0:T(8,128)(2,1)S(1)} all-to-all(bf16[8,64,512]{2,1,0:T(8,128)(2,1)S(1)} %shard_map.88), channel_id=1, replica_groups=mesh['z'=16,'yh'=4,'yl'=2,'x'=4,'c'=2] {'yl','x'}, dimensions={0} | all-to-all | bytes 1048576 | tf_op jit(solution)/shard_map/all_to_all | solution.py:34
  91.5 0.1 reduce_sum.21
  91.6 17.6 %all_to_all.33 = bf16[16,4,512]{2,1,0:T(4,128)(2,1)S(1)} all-to-all(bf16[16,4,512]{2,1,0:T(4,128)(2,1)S(1)} %reshape.43), channel_id=1, replica_groups=mesh['z'=16,'yh'=4,'yl'=2,'x'=4,'c'=2] {'z'}, dimensions={0} | all-to-all | bytes 131072 | tf_op jit(solution)/shard_map/all_to_all | solution.py:34
  109.2 0.1 convolution_convert_fusion
  109.4 17.3 %all_to_all.34 = bf16[64,4,128]{2,1,0:T(4,128)(2,1)S(1)} all-to-all(bf16[64,4,128]{2,1,0:T(4,128)(2,1)S(1)} %reshape.45), channel_id=1, replica_groups=mesh['z'=16,'yh'=4,'yl'=2,'x'=4,'c'=2] {'yh','yl','x','c'}, dimensions={0} | all-to-all | bytes 131072 | tf_op jit(solution)/shard_map/all_to_all | solution.py:34
  126.7 0.1 reshape.46
  126.8 0.1 reduce_sum.22
  126.9 0.5 slice.20
  127.4 0.6 copy.9
  (7 shorter events, 0.1 us)
Async XLA Ops:
  57.1 3.7 %copy-start = (bf16[1,3584,128]{2,1,0:T(8,128)(2,1)S(1)}, bf16[1,3584,128]{2,1,0:T(8,128)(2,1)}, u32[]{:S(2)}) copy-start(bf16[1,3584,128]{2,1,0:T(8,128)(2,1)} %param.11) | copy-start | bytes 2752516
  57.1 8.9 %copy-start.1 = (bf16[1,3584,128]{2,1,0:T(8,128)(2,1)S(1)}, bf16[1,3584,128]{2,1,0:T(8,128)(2,1)}, u32[]{:S(2)}) copy-start(bf16[1,3584,128]{2,1,0:T(8,128)(2,1)} %param.12) | copy-start | bytes 2752516
  57.1 15.6 %all-to-all-start.2 = ((bf16[8,64,896]{2,1,0:T(8,128)(2,1)}), bf16[8,64,896]{2,1,0:T(8,128)(2,1)S(1)}, u32[]{:S(2)}, u32[]{:S(2)}) async-start(bf16[8,64,896]{2,1,0:T(8,128)(2,1)} %broadcast_in_dim.2), calls=%async_computation.2 | async-start | bytes 1835008 | tf_op jit(solution)/shard_map/all_to_all | solution.py:34
  60.8 9.5 %collective-permute-start = (bf16[3584,128]{1,0:T(8,128)(2,1)S(1)}, bf16[3584,128]{1,0:T(8,128)(2,1)S(1)}, u32[]{:S(2)}, u32[]{:S(2)}) collective-permute-start(bf16[3584,128]{1,0:T(8,128)(2,1)S(1)} %bitcast.10), channel_id=1, source_target_pairs={{0,1},{1,0},{2,3},{3,2},{4,5},{5,4},{6,7},{7,6},{8,9},{9,8},{10,11... | collective-permute-start | bytes 2752520 | tf_op jit(solution)/shard_map/ppermute | solution.py:161
  66.0 4.4 %collective-permute-start.1 = (bf16[3584,128]{1,0:T(8,128)(2,1)S(1)}, bf16[3584,128]{1,0:T(8,128)(2,1)S(1)}, u32[]{:S(2)}, u32[]{:S(2)}) collective-permute-start(bf16[3584,128]{1,0:T(8,128)(2,1)S(1)} %bitcast.14), channel_id=1, source_target_pairs={{0,1},{1,0},{2,3},{3,2},{4,5},{5,4},{6,7},{7,6},{8,9},{9,8},{10,11... | collective-permute-start | bytes 2752520 | tf_op jit(solution)/shard_map/ppermute | solution.py:161
  67.9 4.8 %collective-permute-start.2 = (bf16[128,3584]{1,0:T(8,128)(2,1)}, bf16[128,3584]{1,0:T(8,128)(2,1)}, u32[]{:S(2)}, u32[]{:S(2)}) collective-permute-start(bf16[128,3584]{1,0:T(8,128)(2,1)} %bitcast.15), channel_id=1, source_target_pairs={{0,1},{1,0},{2,3},{3,2},{4,5},{5,4},{6,7},{7,6},{8,9},{9,8},{10,11... | collective-permute-start | bytes 2752520 | tf_op jit(solution)/shard_map/ppermute | solution.py:161
  70.3 1.0 copy-start.2
  71.3 0.9 copy-start.3

commit v3 on v2

--- a/solution.py
+++ b/solution.py
@@ -22,7 +22,6 @@
 VMEM = pl.BlockSpec(memory_space=pltpu.VMEM)
 HBM = pl.BlockSpec(memory_space=pltpu.HBM)
 WHOLE = 56
-MOST = 51
 MIB = 1024 * 1024
 
 
@@ -81,11 +80,11 @@
         send_ref[:, k * LANES : (k + 1) * LANES] = dot(place, part, TN).astype(BF16)
 
 
-def expert_kernel(aux_ref, rows_ref, *refs):
-    sources, (out_ref, *weights, arrived) = refs[:6], refs[6:]
+def expert_kernel(aux_ref, rows_ref, wg_ref, wu_ref, wd_ref, *refs):
+    sources, (out_ref, *others, arrived) = refs[:3], refs[3:]
     copies = [
         pltpu.make_async_copy(source, target, arrived.at[i])
-        for i, (source, target) in enumerate(zip(sources, weights))
+        for i, (source, target) in enumerate(zip(sources, others))
     ]
     for copy in copies:
         copy.start()
@@ -96,28 +95,26 @@
     prob = jnp.sum(prob, axis=1, keepdims=True)
     gate_terms = jnp.zeros((rows, 1), F32)
     grads = []
-    for core in range(2):
-        gate_w, up_w, down_w = weights[3 * core : 3 * core + 3]
-        for copy in copies[3 * core : 3 * core + 3]:
-            copy.wait()
-        gate = jnp.zeros((rows, LANES), F32)
-        up = jnp.zeros((rows, LANES), F32)
-        back = jnp.zeros((rows, LANES), F32)
-        for i in range(4):
-            at = slice(i * PIECE, (i + 1) * PIECE)
-            gate += dot(rows_ref[i], gate_w[at, :])
-            up += dot(rows_ref[i], up_w[at, :])
-            back += dot(rows_ref[4 + i], down_w[:, at], NT)
+    for core, (gate_w, up_w, down_w) in enumerate(((wg_ref, wu_ref, wd_ref), others)):
+        if core == 1:
+            copies[0].wait()
+            copies[1].wait()
+        both = dot(rows_ref[0], jnp.concatenate([gate_w[...], up_w[...]], axis=1))
+        gate, up = both[:, :LANES], both[:, LANES:]
+        if core == 1:
+            copies[2].wait()
+        back = dot(rows_ref[1], down_w[...], NT)
         logistic = jax.nn.sigmoid(gate)
         swished = gate * logistic
         gate_terms += jnp.sum(swished * up * back, axis=1, keepdims=True)
         scaled = prob * back
         slope = scaled * up * logistic * (1.0 + gate * (1.0 - logistic))
-        grads += [(slope.astype(BF16), gate_w), ((scaled * swished).astype(BF16), up_w)]
+        grads += [slope.astype(BF16), (scaled * swished).astype(BF16)]
+    grad = jnp.concatenate(grads, axis=1)
     for q in range(7):
         at = slice(q * BACK, (q + 1) * BACK)
-        terms = sum(dot(grad, weight[at, :], NT) for grad, weight in grads)
-        out_ref[q] = terms.astype(BF16)
+        weight = [ref[at, :] for ref in (wg_ref, wu_ref, others[0], others[1])]
+        out_ref[q] = dot(grad, jnp.concatenate(weight, axis=1), NT).astype(BF16)
     wide = lax.broadcasted_iota(jnp.int32, (rows, BACK), 1)
     out_ref[7] = jnp.where(wide == column, gate_terms, 0.0).astype(BF16)
 
@@ -160,16 +157,17 @@
 
     others = [lax.ppermute(weight, "c", SWAP) for weight in weights]
     own = exchange(jnp.broadcast_to(rows[None, :, :PIECE], (8, slots, PIECE)), QUAD)
+    own = own.reshape(2, 4, slots, PIECE).transpose(0, 2, 1, 3).reshape(2, slots, width)
     partial = pl.pallas_call(
         expert_kernel,
         out_shape=jax.ShapeDtypeStruct((8, slots, BACK), BF16),
-        in_specs=[VMEM] * 2 + [HBM] * 6,
+        in_specs=[VMEM] * 5 + [HBM] * 3,
         out_specs=VMEM,
         scratch_shapes=[
-            *[pltpu.VMEM(weight.shape, BF16) for weight in (*weights, *weights)],
-            pltpu.SemaphoreType.DMA((6,)),
+            *[pltpu.VMEM(weight.shape, BF16) for weight in weights],
+            pltpu.SemaphoreType.DMA((3,)),
         ],
-        compiler_params=pltpu.CompilerParams(vmem_limit_bytes=MOST * MIB),
+        compiler_params=pltpu.CompilerParams(vmem_limit_bytes=16 * MIB),
         cost_estimate=pl.CostEstimate(
             flops=20 * slots * width * LANES,
             bytes_accessed=8 * MIB,

time: 129 us -> 130 us (level)
  blocking collectives: 102 us -> 104 us
    unnamed x10 -> x8, local copies, waits for them, and re-layouts: 2.51 us -> 0.63 us
    all_to_all x5, blocking collectives: 102 us -> 104 us  [exchange(): return lax.all_to_all(value, axes, split_axis=0, concat_axis=0, tiled=True)]
  transfers between devices with their start and end apart: 4 -> 4, of which waited for: 1 -> 1; matrix products, arithmetic and copies ran while one was open for 0% -> 1% of each run, Pallas kernels for 0% -> 0%
where the time goes in v3:
time: 130 us; the launch traced here: 129 us
  blocking collectives  104 us (80%)
  starting transfers between devices  13.8 us (11%)
  Pallas kernels  6.29 us (5%)
  local copies, waits for them, and re-layouts  3.72 us (3%)
    all_to_all x5, blocking collectives, exchange(): return lax.all_to_all(value, axes, split_axis=0, concat_axis=0, tiled=True)  104 us
    ppermute x3, starting transfers between devices, on_device(): others = [lax.ppermute(weight, 'c', SWAP) for weight in weights]  9.47 us
    all_to_all x1, starting transfers between devices, exchange(): return lax.all_to_all(value, axes, split_axis=0, concat_axis=0, tiled=True)  4.36 us
    pallas_call x1, Pallas kernels, on_device(): pl.pallas_call(expert_kernel, out_shape=jax.ShapeDtypeStruct((8, slots, B...  4.28 us
  transfers between devices with their start and end apart: 4, of which 1 were waited for; matrix products, arithmetic and copies ran while one was open for 1% of the time, Pallas kernels for 0%

profile of v3, /device:TPU:1, one launch (start us, length us, event | category | flops | bytes accessed | tf_op | source)
XLA Modules:
  0.0 129.5 jit_solution(12912719985892125343)
XLA Ops:
  0.6 1.5 %shard_map.86 = bf16[64,8,128]{2,1,0:T(8,128)(2,1)} custom-call(bf16[1,3584]{1,0:T(2,128)(2,1)} %x_hbm.1, bf16[1,3584]{1,0:T(2,128)(2,1)} %dy_hbm.1, bf16[1,8]{1,0:T(2,128)(2,1)} %gate_hbm.1, s32[1,8]{1,0:T(1,128)} %dest_hbm.1), custom_call_target="tpu_custom_call" | custom-call | tf_op jit(solution)/shard_map/pallas_call | solution.py:128
  2.1 29.6 %all_to_all.30 = bf16[64,8,128]{2,1,0:T(8,128)(2,1)S(1)} all-to-all(bf16[64,8,128]{2,1,0:T(8,128)(2,1)} %shard_map.86), channel_id=1, replica_groups=mesh['z'=16,'yh'=4,'yl'=2,'x'=4,'c'=2] {'yh','yl','x','c'}, dimensions={0} | all-to-all | bytes 262144 | tf_op jit(solution)/shard_map/all_to_all | solution.py:33
  31.7 0.5 shard_map.87
  32.3 0.1 reshape.47
  32.3 23.7 %all_to_all.31 = bf16[16,4,1024]{2,1,0:T(4,128)(2,1)S(1)} all-to-all(bf16[16,4,1024]{2,1,0:T(4,128)(2,1)S(1)} %reshape.47), channel_id=1, replica_groups=mesh['z'=16,'yh'=4,'yl'=2,'x'=4,'c'=2] {'z'}, dimensions={0} | all-to-all | bytes 262144 | tf_op jit(solution)/shard_map/all_to_all | solution.py:33
  56.0 0.0 copy-start.2
  56.1 1.1 broadcast_in_dim.2
  57.1 0.0 copy-start
  57.1 0.0 copy-start.1
  57.1 4.4 %all-to-all-start.2 = ((bf16[8,64,896]{2,1,0:T(8,128)(2,1)}), bf16[8,64,896]{2,1,0:T(8,128)(2,1)}, u32[]{:S(2)}, u32[]{:S(2)}) async-start(bf16[8,64,896]{2,1,0:T(8,128)(2,1)} %broadcast_in_dim.2), calls=%async_computation.2 | async-start | bytes 1835008 | tf_op jit(solution)/shard_map/all_to_all | solution.py:33
  61.5 0.0 copy-done
  61.5 5.1 %collective-permute-start = (bf16[3584,128]{1,0:T(8,128)(2,1)S(1)}, bf16[3584,128]{1,0:T(8,128)(2,1)}, u32[]{:S(2)}, u32[]{:S(2)}) collective-permute-start(bf16[3584,128]{1,0:T(8,128)(2,1)S(1)} %bitcast.16), channel_id=1, source_target_pairs={{0,1},{1,0},{2,3},{3,2},{4,5},{5,4},{6,7},{7,6},{8,9},{9,8},{10,11... | collective-permute-start | bytes 2752520 | tf_op jit(solution)/shard_map/ppermute | solution.py:158
  66.7 0.0 copy-done.1
  66.7 1.9 %collective-permute-start.1 = (bf16[3584,128]{1,0:T(8,128)(2,1)S(1)}, bf16[3584,128]{1,0:T(8,128)(2,1)}, u32[]{:S(2)}, u32[]{:S(2)}) collective-permute-start(bf16[3584,128]{1,0:T(8,128)(2,1)S(1)} %bitcast.18), channel_id=1, source_target_pairs={{0,1},{1,0},{2,3},{3,2},{4,5},{5,4},{6,7},{7,6},{8,9},{9,8},{10,11... | collective-permute-start | bytes 2752520 | tf_op jit(solution)/shard_map/ppermute | solution.py:158
  68.6 0.0 copy-done.2
  68.6 2.4 %collective-permute-start.2 = (bf16[128,3584]{1,0:T(8,128)(2,1)S(1)}, bf16[128,3584]{1,0:T(8,128)(2,1)}, u32[]{:S(2)}, u32[]{:S(2)}) collective-permute-start(bf16[128,3584]{1,0:T(8,128)(2,1)S(1)} %bitcast.20), channel_id=1, source_target_pairs={{0,1},{1,0},{2,3},{3,2},{4,5},{5,4},{6,7},{7,6},{8,9},{9,8},{10,11... | collective-permute-start | bytes 2752520 | tf_op jit(solution)/shard_map/ppermute | solution.py:158
  71.0 0.0 all-to-all-done.2
  71.0 1.3 copy.10
  72.3 0.0 collective-permute-done.refs_0_
  72.3 0.0 collective-permute-done.1.refs_1_
  72.3 0.9 collective-permute-done.2.refs_2_
  73.2 4.3 %shard_map.88 = bf16[8,64,512]{2,1,0:T(8,128)(2,1)S(1)} custom-call(bf16[64,128]{1,0:T(8,128)(2,1)S(1)} %slice.17.aux_ref, bf16[2,64,3584]{2,1,0:T(8,128)(2,1)S(1)} %bitcast.15, bf16[3584,128]{1,0:T(8,128)(2,1)S(1)} %bitcast.17, bf16[3584,128]{1,0:T(8,128)(2,1)S(1)} %bitcast.19, bf16[128,3584]{1,0:T(8,128)(2,1)S(1)} %bitcast.21, ...), custom_call_target="tpu_custom_call" | custom-call | flops 587202560 | bytes 8388608 | tf_op jit(solution)/shard_map/pallas_call | solution.py:161
  77.5 13.8 %all_to_all.32 = bf16[8,64,512]{2,1,0:T(8,128)(2,1)S(1)} all-to-all(bf16[8,64,512]{2,1,0:T(8,128)(2,1)S(1)} %shard_map.88), channel_id=1, replica_groups=mesh['z'=16,'yh'=4,'yl'=2,'x'=4,'c'=2] {'yl','x'}, dimensions={0} | all-to-all | bytes 1048576 | tf_op jit(solution)/shard_map/all_to_all | solution.py:33
  91.3 0.1 reduce_sum.21
  91.4 19.3 %all_to_all.33 = bf16[16,4,512]{2,1,0:T(4,128)(2,1)S(1)} all-to-all(bf16[16,4,512]{2,1,0:T(4,128)(2,1)S(1)} %reshape.51), channel_id=1, replica_groups=mesh['z'=16,'yh'=4,'yl'=2,'x'=4,'c'=2] {'z'}, dimensions={0} | all-to-all | bytes 131072 | tf_op jit(solution)/shard_map/all_to_all | solution.py:33
  110.7 0.1 convolution_convert_fusion
  110.9 17.3 %all_to_all.34 = bf16[64,4,128]{2,1,0:T(4,128)(2,1)S(1)} all-to-all(bf16[64,4,128]{2,1,0:T(4,128)(2,1)S(1)} %reshape.53), channel_id=1, replica_groups=mesh['z'=16,'yh'=4,'yl'=2,'x'=4,'c'=2] {'yh','yl','x','c'}, dimensions={0} | all-to-all | bytes 131072 | tf_op jit(solution)/shard_map/all_to_all | solution.py:33
  128.2 0.1 reshape.54
  128.3 0.1 reduce_sum.22
  128.4 0.5 slice.20
  128.9 0.6 copy.11
  (7 shorter events, 0.1 us)
Async XLA Ops:
  56.0 12.6 %copy-start.2 = (bf16[1,128,3584]{2,1,0:T(8,128)(2,1)S(1)}, bf16[1,128,3584]{2,1,0:T(8,128)(2,1)}, u32[]{:S(2)}) copy-start(bf16[1,128,3584]{2,1,0:T(8,128)(2,1)} %param.13) | copy-start | bytes 2752516
  57.1 4.4 %copy-start = (bf16[1,3584,128]{2,1,0:T(8,128)(2,1)S(1)}, bf16[1,3584,128]{2,1,0:T(8,128)(2,1)}, u32[]{:S(2)}) copy-start(bf16[1,3584,128]{2,1,0:T(8,128)(2,1)} %param.11) | copy-start | bytes 2752516
  57.1 9.5 %copy-start.1 = (bf16[1,3584,128]{2,1,0:T(8,128)(2,1)S(1)}, bf16[1,3584,128]{2,1,0:T(8,128)(2,1)}, u32[]{:S(2)}) copy-start(bf16[1,3584,128]{2,1,0:T(8,128)(2,1)} %param.12) | copy-start | bytes 2752516
  57.1 13.9 %all-to-all-start.2 = ((bf16[8,64,896]{2,1,0:T(8,128)(2,1)}), bf16[8,64,896]{2,1,0:T(8,128)(2,1)}, u32[]{:S(2)}, u32[]{:S(2)}) async-start(bf16[8,64,896]{2,1,0:T(8,128)(2,1)} %broadcast_in_dim.2), calls=%async_computation.2 | async-start | bytes 1835008 | tf_op jit(solution)/shard_map/all_to_all | solution.py:33
  61.5 10.8 %collective-permute-start = (bf16[3584,128]{1,0:T(8,128)(2,1)S(1)}, bf16[3584,128]{1,0:T(8,128)(2,1)}, u32[]{:S(2)}, u32[]{:S(2)}) collective-permute-start(bf16[3584,128]{1,0:T(8,128)(2,1)S(1)} %bitcast.16), channel_id=1, source_target_pairs={{0,1},{1,0},{2,3},{3,2},{4,5},{5,4},{6,7},{7,6},{8,9},{9,8},{10,11... | collective-permute-start | bytes 2752520 | tf_op jit(solution)/shard_map/ppermute | solution.py:158
  66.7 5.7 %collective-permute-start.1 = (bf16[3584,128]{1,0:T(8,128)(2,1)S(1)}, bf16[3584,128]{1,0:T(8,128)(2,1)}, u32[]{:S(2)}, u32[]{:S(2)}) collective-permute-start(bf16[3584,128]{1,0:T(8,128)(2,1)S(1)} %bitcast.18), channel_id=1, source_target_pairs={{0,1},{1,0},{2,3},{3,2},{4,5},{5,4},{6,7},{7,6},{8,9},{9,8},{10,11... | collective-permute-start | bytes 2752520 | tf_op jit(solution)/shard_map/ppermute | solution.py:158
  68.6 4.6 %collective-permute-start.2 = (bf16[128,3584]{1,0:T(8,128)(2,1)S(1)}, bf16[128,3584]{1,0:T(8,128)(2,1)}, u32[]{:S(2)}, u32[]{:S(2)}) collective-permute-start(bf16[128,3584]{1,0:T(8,128)(2,1)S(1)} %bitcast.20), channel_id=1, source_target_pairs={{0,1},{1,0},{2,3},{3,2},{4,5},{5,4},{6,7},{7,6},{8,9},{9,8},{10,11... | collective-permute-start | bytes 2752520 | tf_op jit(solution)/shard_map/ppermute | solution.py:158

commit v4 on v3

--- a/solution.py
+++ b/solution.py
@@ -54,6 +54,22 @@
         for pair in range(4):
             for core in range(2):
                 out_ref[pair * 16 + q * 2 + core] = tile
+
+
+def weights_kernel(wg_ref, wu_ref, wd_ref, after_ref, out_ref, arrived):
+    width = wg_ref.shape[0]
+    pairs = [(wg_ref, out_ref.at[:width, :]), (wu_ref, out_ref.at[width : 2 * width, :])]
+    for k in range(width // LANES):
+        at = slice(k * LANES, (k + 1) * LANES)
+        pairs.append((wd_ref.at[:, at], out_ref.at[2 * width + k * LANES : 2 * width + (k + 1) * LANES, :]))
+    copies = [
+        pltpu.make_async_copy(source, target, arrived.at[i])
+        for i, (source, target) in enumerate(pairs)
+    ]
+    for copy in copies:
+        copy.start()
+    for copy in copies:
+        copy.wait()
 
 
 def place_kernel(got_ref, send_ref, place_ref, wide):
@@ -80,30 +96,31 @@
         send_ref[:, k * LANES : (k + 1) * LANES] = dot(place, part, TN).astype(BF16)
 
 
-def expert_kernel(aux_ref, rows_ref, wg_ref, wu_ref, wd_ref, *refs):
-    sources, (out_ref, *others, arrived) = refs[:3], refs[3:]
-    copies = [
-        pltpu.make_async_copy(source, target, arrived.at[i])
-        for i, (source, target) in enumerate(zip(sources, others))
-    ]
-    for copy in copies:
-        copy.start()
+def expert_kernel(aux_ref, rows_ref, wg_ref, wu_ref, wd_ref, theirs_ref, out_ref, other_ref, arrived):
+    copy = pltpu.make_async_copy(theirs_ref, other_ref, arrived)
+    copy.start()
+    width = wg_ref.shape[0]
     column = 2 * lax.axis_index("yh") + lax.axis_index("yl")
     rows = rows_ref.shape[1]
     lane = lax.broadcasted_iota(jnp.int32, (rows, LANES), 1)
     prob = jnp.where(lane == column, aux_ref[...].astype(F32), 0.0)
     prob = jnp.sum(prob, axis=1, keepdims=True)
+    x = jnp.concatenate([rows_ref[i] for i in range(4)], axis=1)
+    dy = jnp.concatenate([rows_ref[i] for i in range(4, 8)], axis=1)
     gate_terms = jnp.zeros((rows, 1), F32)
     grads = []
-    for core, (gate_w, up_w, down_w) in enumerate(((wg_ref, wu_ref, wd_ref), others)):
-        if core == 1:
-            copies[0].wait()
-            copies[1].wait()
-        both = dot(rows_ref[0], jnp.concatenate([gate_w[...], up_w[...]], axis=1))
+    for core in range(2):
+        if core == 0:
+            gate_up = jnp.concatenate([wg_ref[...], wu_ref[...]], axis=1)
+            down = wd_ref[...]
+        else:
+            copy.wait()
+            gate_up = jnp.concatenate([other_ref[:width, :], other_ref[width : 2 * width, :]], axis=1)
+            tiles = range(2 * width, 3 * width, LANES)
+            down = jnp.concatenate([other_ref[k : k + LANES, :] for k in tiles], axis=1)
+        both = dot(x, gate_up)
         gate, up = both[:, :LANES], both[:, LANES:]
-        if core == 1:
-            copies[2].wait()
-        back = dot(rows_ref[1], down_w[...], NT)
+        back = dot(dy, down, NT)
         logistic = jax.nn.sigmoid(gate)
         swished = gate * logistic
         gate_terms += jnp.sum(swished * up * back, axis=1, keepdims=True)
@@ -113,7 +130,8 @@
     grad = jnp.concatenate(grads, axis=1)
     for q in range(7):
         at = slice(q * BACK, (q + 1) * BACK)
-        weight = [ref[at, :] for ref in (wg_ref, wu_ref, others[0], others[1])]
+        beyond = slice(width + q * BACK, width + (q + 1) * BACK)
+        weight = [wg_ref[at, :], wu_ref[at, :], other_ref[at, :], other_ref[beyond, :]]
         out_ref[q] = dot(grad, jnp.concatenate(weight, axis=1), NT).astype(BF16)
     wide = lax.broadcasted_iota(jnp.int32, (rows, BACK), 1)
     out_ref[7] = jnp.where(wide == column, gate_terms, 0.0).astype(BF16)
@@ -140,6 +158,17 @@
         compiler_params=pltpu.CompilerParams(vmem_limit_bytes=WHOLE * MIB),
     )(tokens, out_grad, gate_prob, dest_node)
     got = exchange(out, LOCAL)
+    packed = pl.pallas_call(
+        weights_kernel,
+        out_shape=jax.ShapeDtypeStruct((3 * width, LANES), BF16),
+        in_specs=[HBM] * 4,
+        out_specs=HBM,
+        scratch_shapes=[pltpu.SemaphoreType.DMA((2 + width // LANES,))],
+        compiler_params=pltpu.CompilerParams(vmem_limit_bytes=WHOLE * MIB),
+        cost_estimate=pl.CostEstimate(flops=0, bytes_accessed=6 * MIB, transcendentals=0),
+    )(*weights, out)
+    got, packed = lax.optimization_barrier((got, packed))
+    other = lax.ppermute(packed, "c", SWAP)
 
     send, place = pl.pallas_call(
         place_kernel,
@@ -153,27 +182,24 @@
         compiler_params=pltpu.CompilerParams(vmem_limit_bytes=4 * MIB),
     )(got.reshape(64 * 8, LANES))
     rows = exchange(send[:slots].reshape(nodes, HALF, PIECE + LANES), "z")
-    rows = rows.reshape(slots, PIECE + LANES)
-
-    others = [lax.ppermute(weight, "c", SWAP) for weight in weights]
-    own = exchange(jnp.broadcast_to(rows[None, :, :PIECE], (8, slots, PIECE)), QUAD)
-    own = own.reshape(2, 4, slots, PIECE).transpose(0, 2, 1, 3).reshape(2, slots, width)
+    rows, other = lax.optimization_barrier((rows.reshape(slots, PIECE + LANES), other))
+
+    aux, spread = rows[:, PIECE:], jnp.broadcast_to(rows[None, :, :PIECE], (8, slots, PIECE))
+    aux, spread = lax.optimization_barrier((aux, spread))
+    own = exchange(spread, QUAD)
     partial = pl.pallas_call(
         expert_kernel,
         out_shape=jax.ShapeDtypeStruct((8, slots, BACK), BF16),
-        in_specs=[VMEM] * 5 + [HBM] * 3,
+        in_specs=[VMEM] * 5 + [HBM],
         out_specs=VMEM,
-        scratch_shapes=[
-            *[pltpu.VMEM(weight.shape, BF16) for weight in weights],
-            pltpu.SemaphoreType.DMA((3,)),
-        ],
+        scratch_shapes=[pltpu.VMEM((3 * width, LANES), BF16), pltpu.SemaphoreType.DMA],
         compiler_params=pltpu.CompilerParams(vmem_limit_bytes=16 * MIB),
         cost_estimate=pl.CostEstimate(
             flops=20 * slots * width * LANES,
             bytes_accessed=8 * MIB,
             transcendentals=2 * slots * LANES,
         ),
-    )(rows[:, PIECE:], own, *weights, *others)
+    )(aux, own, *weights, other)
 
     terms = exchange(partial, QUAD)
     summed = jnp.sum(terms.astype(F32), axis=0).astype(BF16)

time: 130 us -> 207 us (1.59)
  Pallas kernels: 6.29 us -> 91 us
  blocking collectives: 104 us -> 91.6 us
  starting transfers between devices: 13.8 us -> 21 us
  local copies, waits for them, and re-layouts: 3.72 us -> 1.51 us
    pallas_call x0 -> x1, Pallas kernels: none -> 84.8 us  [on_device(): pl.pallas_call(weights_kernel, out_shape=jax.ShapeDtypeStruct((3 * width,...]
    all_to_all x1, starting transfers between devices: 4.36 us -> 18.2 us  [exchange(): return lax.all_to_all(value, axes, split_axis=0, concat_axis=0, tiled=True)]
    all_to_all x5, blocking collectives: 104 us -> 91.6 us  [exchange(): return lax.all_to_all(value, axes, split_axis=0, concat_axis=0, tiled=True)]
    ppermute x3 -> x1, starting transfers between devices: 9.47 us -> 2.74 us  [on_device(): other = lax.ppermute(packed, 'c', SWAP)]
  transfers between devices with their start and end apart: 4 -> 2, of which waited for: 1 -> 0; matrix products, arithmetic and copies ran while one was open for 1% -> 0% of each run, Pallas kernels for 0% -> 41%
where the time goes in v4:
time: 207 us; the launch traced here: 206 us
  blocking collectives  91.6 us (44%)
  Pallas kernels  91 us (44%)
  starting transfers between devices  21 us (10%)
    all_to_all x5, blocking collectives, exchange(): return lax.all_to_all(value, axes, split_axis=0, concat_axis=0, tiled=True)  91.6 us
    pallas_call x1, Pallas kernels, on_device(): pl.pallas_call(weights_kernel, out_shape=jax.ShapeDtypeStruct((3 * width,...  84.8 us
    all_to_all x1, starting transfers between devices, exchange(): return lax.all_to_all(value, axes, split_axis=0, concat_axis=0, tiled=True)  18.2 us
    pallas_call x1, Pallas kernels, on_device(): pl.pallas_call(expert_kernel, out_shape=jax.ShapeDtypeStruct((8, slots, B...  4.26 us
  transfers between devices with their start and end apart: 2, of which 0 were waited for; matrix products, arithmetic and copies ran while one was open for 0% of the time, Pallas kernels for 41%

profile of v4, /device:TPU:1, one launch (start us, length us, event | category | flops | bytes accessed | tf_op | source)
XLA Modules:
  0.0 206.2 jit_solution(2705201009410715659)
XLA Ops:
  0.6 1.5 shard_map.86.after_ref
  2.1 18.2 %all-to-all-start = ((bf16[64,8,128]{2,1,0:T(8,128)(2,1)}), bf16[64,8,128]{2,1,0:T(8,128)(2,1)S(1)}, u32[]{:S(2)}, u32[]{:S(2)}) async-start(bf16[64,8,128]{2,1,0:T(8,128)(2,1)} %shard_map.86.after_ref), calls=%async_computation | async-start | bytes 262144 | tf_op jit(solution)/shard_map/all_to_all | solution.py:33
  20.4 84.8 %shard_map.87 = bf16[10752,128]{1,0:T(8,128)(2,1)} custom-call(bf16[3584,128]{1,0:T(8,128)(2,1)} %bitcast.10, bf16[3584,128]{1,0:T(8,128)(2,1)} %bitcast.12, bf16[128,3584]{1,0:T(8,128)(2,1)} %bitcast.14, bf16[64,8,128]{2,1,0:T(8,128)(2,1)} %shard_map.86.after_ref), custom_call_target="tpu_custom_call" | custom-call | bytes 6291456 | tf_op jit(solution)/shard_map/pallas_call | solution.py:161
  105.1 0.0 copy-start
  105.1 0.0 copy-start.1
  105.2 0.0 copy-start.2
  105.2 0.0 all-to-all-done
  105.2 2.7 %collective-permute-start = (bf16[10752,128]{1,0:T(8,128)(2,1)}, bf16[10752,128]{1,0:T(8,128)(2,1)}, u32[]{:S(2)}, u32[]{:S(2)}) collective-permute-start(bf16[10752,128]{1,0:T(8,128)(2,1)} %shard_map.87), channel_id=1, source_target_pairs={{0,1},{1,0},{2,3},{3,2},{4,5},{5,4},{6,7},{7,6},{8,9},{9,8},{10,11... | collective-permute-start | bytes 8257544 | tf_op jit(solution)/shard_map/ppermute | solution.py:171
  107.9 0.5 shard_map.88
  108.5 0.1 reshape.41
  108.5 24.0 %all_to_all.30 = bf16[16,4,1024]{2,1,0:T(4,128)(2,1)S(1)} all-to-all(bf16[16,4,1024]{2,1,0:T(4,128)(2,1)S(1)} %reshape.41), channel_id=1, replica_groups=mesh['z'=16,'yh'=4,'yl'=2,'x'=4,'c'=2] {'z'}, dimensions={0} | all-to-all | bytes 262144 | tf_op jit(solution)/shard_map/all_to_all | solution.py:33
  132.6 0.0 collective-permute-done.theirs_ref
  132.6 0.1 broadcast_in_dim.2
  132.7 15.4 %all_to_all.31.rows_ref = bf16[8,64,896]{2,1,0:T(8,128)(2,1)S(1)} all-to-all(bf16[8,64,896]{2,1,0:T(8,128)(2,1)S(1)} %broadcast_in_dim.2), channel_id=1, replica_groups=mesh['z'=16,'yh'=4,'yl'=2,'x'=4,'c'=2] {'yl','x'}, dimensions={0} | all-to-all | bytes 1835008 | tf_op jit(solution)/shard_map/all_to_all | solution.py:33
  148.2 0.0 copy-done
  148.2 0.0 copy-done.1
  148.2 0.0 copy-done.2
  148.2 4.3 %shard_map.89 = bf16[8,64,512]{2,1,0:T(8,128)(2,1)S(1)} custom-call(bf16[64,128]{1,0:T(8,128)(2,1)S(1)} %slice.13.aux_ref, bf16[8,64,896]{2,1,0:T(8,128)(2,1)S(1)} %all_to_all.31.rows_ref, bf16[3584,128]{1,0:T(8,128)(2,1)S(1)} %bitcast.11, bf16[3584,128]{1,0:T(8,128)(2,1)S(1)} %bitcast.13, bf16[128,3584]{1,0:T(8,128)(2,1)S(1)} %bitcast.15, ...), custom_call_target="tpu_custom_call" | custom-call | flops 587202560 | bytes 8388608 | tf_op jit(solution)/shard_map/pallas_call | solution.py:190
  152.4 11.0 %all_to_all.32 = bf16[8,64,512]{2,1,0:T(8,128)(2,1)S(1)} all-to-all(bf16[8,64,512]{2,1,0:T(8,128)(2,1)S(1)} %shard_map.89), channel_id=1, replica_groups=mesh['z'=16,'yh'=4,'yl'=2,'x'=4,'c'=2] {'yl','x'}, dimensions={0} | all-to-all | bytes 1048576 | tf_op jit(solution)/shard_map/all_to_all | solution.py:33
  163.4 0.1 reduce_sum.21
  163.5 19.6 %all_to_all.33 = bf16[16,4,512]{2,1,0:T(4,128)(2,1)S(1)} all-to-all(bf16[16,4,512]{2,1,0:T(4,128)(2,1)S(1)} %reshape.43), channel_id=1, replica_groups=mesh['z'=16,'yh'=4,'yl'=2,'x'=4,'c'=2] {'z'}, dimensions={0} | all-to-all | bytes 131072 | tf_op jit(solution)/shard_map/all_to_all | solution.py:33
  183.2 0.1 convolution_convert_fusion
  183.3 21.6 %all_to_all.34 = bf16[64,4,128]{2,1,0:T(4,128)(2,1)S(1)} all-to-all(bf16[64,4,128]{2,1,0:T(4,128)(2,1)S(1)} %reshape.45), channel_id=1, replica_groups=mesh['z'=16,'yh'=4,'yl'=2,'x'=4,'c'=2] {'yh','yl','x','c'}, dimensions={0} | all-to-all | bytes 131072 | tf_op jit(solution)/shard_map/all_to_all | solution.py:33
  204.9 0.1 reshape.46
  205.0 0.1 reduce_sum.22
  205.1 0.5 slice.18
  205.6 0.6 copy.9
  (7 shorter events, 0.1 us)
Async XLA Ops:
  2.1 103.0 %all-to-all-start = ((bf16[64,8,128]{2,1,0:T(8,128)(2,1)}), bf16[64,8,128]{2,1,0:T(8,128)(2,1)S(1)}, u32[]{:S(2)}, u32[]{:S(2)}) async-start(bf16[64,8,128]{2,1,0:T(8,128)(2,1)} %shard_map.86.after_ref), calls=%async_computation | async-start | bytes 262144 | tf_op jit(solution)/shard_map/all_to_all | solution.py:33
  105.1 43.0 %copy-start = (bf16[1,3584,128]{2,1,0:T(8,128)(2,1)S(1)}, bf16[1,3584,128]{2,1,0:T(8,128)(2,1)}, u32[]{:S(2)}) copy-start(bf16[1,3584,128]{2,1,0:T(8,128)(2,1)} %param.11) | copy-start | bytes 2752516
  105.1 43.0 %copy-start.1 = (bf16[1,3584,128]{2,1,0:T(8,128)(2,1)S(1)}, bf16[1,3584,128]{2,1,0:T(8,128)(2,1)}, u32[]{:S(2)}) copy-start(bf16[1,3584,128]{2,1,0:T(8,128)(2,1)} %param.12) | copy-start | bytes 2752516
  105.2 43.0 %copy-start.2 = (bf16[1,128,3584]{2,1,0:T(8,128)(2,1)S(1)}, bf16[1,128,3584]{2,1,0:T(8,128)(2,1)}, u32[]{:S(2)}) copy-start(bf16[1,128,3584]{2,1,0:T(8,128)(2,1)} %param.13) | copy-start | bytes 2752516
  105.2 27.4 %collective-permute-start = (bf16[10752,128]{1,0:T(8,128)(2,1)}, bf16[10752,128]{1,0:T(8,128)(2,1)}, u32[]{:S(2)}, u32[]{:S(2)}) collective-permute-start(bf16[10752,128]{1,0:T(8,128)(2,1)} %shard_map.87), channel_id=1, source_target_pairs={{0,1},{1,0},{2,3},{3,2},{4,5},{5,4},{6,7},{7,6},{8,9},{9,8},{10,11... | collective-permute-start | bytes 8257544 | tf_op jit(solution)/shard_map/ppermute | solution.py:171

commit v5 on v2

--- a/solution.py
+++ b/solution.py
@@ -94,32 +94,42 @@
     lane = lax.broadcasted_iota(jnp.int32, (rows, LANES), 1)
     prob = jnp.where(lane == column, aux_ref[...].astype(F32), 0.0)
     prob = jnp.sum(prob, axis=1, keepdims=True)
+    x = jnp.concatenate([rows_ref[i] for i in range(4)], axis=1)
+    dy = jnp.concatenate([rows_ref[i] for i in range(4, 8)], axis=1)
     gate_terms = jnp.zeros((rows, 1), F32)
     grads = []
     for core in range(2):
-        gate_w, up_w, down_w = weights[3 * core : 3 * core + 3]
         for copy in copies[3 * core : 3 * core + 3]:
             copy.wait()
-        gate = jnp.zeros((rows, LANES), F32)
-        up = jnp.zeros((rows, LANES), F32)
-        back = jnp.zeros((rows, LANES), F32)
-        for i in range(4):
-            at = slice(i * PIECE, (i + 1) * PIECE)
-            gate += dot(rows_ref[i], gate_w[at, :])
-            up += dot(rows_ref[i], up_w[at, :])
-            back += dot(rows_ref[4 + i], down_w[:, at], NT)
+        gate_w, up_w, down_w = weights[3 * core : 3 * core + 3]
+        both = dot(x, jnp.concatenate([gate_w[...], up_w[...]], axis=1))
+        gate, up = both[:, :LANES], both[:, LANES:]
+        back = dot(dy, down_w[...], NT)
         logistic = jax.nn.sigmoid(gate)
         swished = gate * logistic
         gate_terms += jnp.sum(swished * up * back, axis=1, keepdims=True)
         scaled = prob * back
         slope = scaled * up * logistic * (1.0 + gate * (1.0 - logistic))
-        grads += [(slope.astype(BF16), gate_w), ((scaled * swished).astype(BF16), up_w)]
+        grads += [slope.astype(BF16), (scaled * swished).astype(BF16)]
+    grad = jnp.concatenate(grads, axis=1)
     for q in range(7):
         at = slice(q * BACK, (q + 1) * BACK)
-        terms = sum(dot(grad, weight[at, :], NT) for grad, weight in grads)
-        out_ref[q] = terms.astype(BF16)
-    wide = lax.broadcasted_iota(jnp.int32, (rows, BACK), 1)
-    out_ref[7] = jnp.where(wide == column, gate_terms, 0.0).astype(BF16)
+        wide = [weights[i][at, :] for i in (0, 1, 3, 4)]
+        out_ref[q] = dot(grad, jnp.concatenate(wide, axis=1), NT).astype(BF16)
+    lane = lax.broadcasted_iota(jnp.int32, (rows, BACK), 1)
+    out_ref[7] = jnp.where(lane == column, gate_terms, 0.0).astype(BF16)
+
+
+def sum_kernel(home_ref, grad_ref, gate_ref):
+    for q in range(8):
+        parts = [home_ref[pair * 16 + q * 2 + core].astype(F32) for pair in range(4) for core in range(2)]
+        total = sum(parts)
+        if q == 7:
+            gate_ref[...] = total[:1, :8]
+        else:
+            for k in range(BACK // LANES):
+                at = q * BACK + k * LANES
+                grad_ref[:, at : at + LANES] = total[k : k + 1, :].astype(BF16)
 
 
 def on_device(tokens, out_grad, gate_prob, dest_node, w_gate, w_up, w_down):
@@ -183,8 +193,16 @@
     back = exchange(summed.reshape(nodes, HALF, BACK), "z").reshape(slots, BACK)
     chosen = dot(place[:, :slots], back).astype(BF16)
     home = exchange(chosen.reshape(64, BACK // LANES, LANES), LOCAL)
-    total = jnp.sum(home.reshape(4, 8, 2, BACK).astype(F32), axis=(0, 2))
-    return total[:7].reshape(1, width).astype(BF16), total[7:, :8]
+    return pl.pallas_call(
+        sum_kernel,
+        out_shape=(
+            jax.ShapeDtypeStruct((1, width), BF16),
+            jax.ShapeDtypeStruct((1, 8), F32),
+        ),
+        in_specs=[VMEM],
+        out_specs=(VMEM, VMEM),
+        compiler_params=pltpu.CompilerParams(vmem_limit_bytes=4 * MIB),
+    )(home)
 
 
 def solution(mesh):

time: 129 us -> 127 us (0.984)
  no operation moved by 1% of the time
where the time goes in v5:
time: 127 us
  blocking collectives  102 us (80%)
  starting transfers between devices  13.2 us (10%)
  Pallas kernels  7.1 us (6%)
  local copies, waits for them, and re-layouts  3.14 us (2%)
    all_to_all x5, blocking collectives, exchange(): return lax.all_to_all(value, axes, split_axis=0, concat_axis=0, tiled=True)  102 us
    ppermute x3, starting transfers between devices, on_device(): others = [lax.ppermute(weight, 'c', SWAP) for weight in weights]  9.47 us
    pallas_call x1, Pallas kernels, on_device(): pl.pallas_call(expert_kernel, out_shape=jax.ShapeDtypeStruct((8, slots, B...  4.44 us
    all_to_all x1, starting transfers between devices, exchange(): return lax.all_to_all(value, axes, split_axis=0, concat_axis=0, tiled=True)  3.68 us
  transfers between devices with their start and end apart: 4, of which 1 were waited for; matrix products, arithmetic and copies ran while one was open for 0% of the time, Pallas kernels for 0%

profile of v5, /device:TPU:1, one launch (start us, length us, event | category | flops | bytes accessed | tf_op | source)
XLA Modules:
  0.0 126.9 jit_solution(8291365452405392603)
XLA Ops:
  0.6 1.5 %shard_map.86 = bf16[64,8,128]{2,1,0:T(8,128)(2,1)} custom-call(bf16[1,3584]{1,0:T(2,128)(2,1)} %x_hbm.1, bf16[1,3584]{1,0:T(2,128)(2,1)} %dy_hbm.1, bf16[1,8]{1,0:T(2,128)(2,1)} %gate_hbm.1, s32[1,8]{1,0:T(1,128)} %dest_hbm.1), custom_call_target="tpu_custom_call" | custom-call | tf_op jit(solution)/shard_map/pallas_call | solution.py:141
  2.1 29.6 %all_to_all.30 = bf16[64,8,128]{2,1,0:T(8,128)(2,1)S(1)} all-to-all(bf16[64,8,128]{2,1,0:T(8,128)(2,1)} %shard_map.86), channel_id=1, replica_groups=mesh['z'=16,'yh'=4,'yl'=2,'x'=4,'c'=2] {'yh','yl','x','c'}, dimensions={0} | all-to-all | bytes 262144 | tf_op jit(solution)/shard_map/all_to_all | solution.py:34
  31.8 0.5 shard_map.87
  32.3 0.1 reshape.24
  32.3 23.7 %all_to_all.31 = bf16[16,4,1024]{2,1,0:T(4,128)(2,1)S(1)} all-to-all(bf16[16,4,1024]{2,1,0:T(4,128)(2,1)S(1)} %reshape.24), channel_id=1, replica_groups=mesh['z'=16,'yh'=4,'yl'=2,'x'=4,'c'=2] {'z'}, dimensions={0} | all-to-all | bytes 262144 | tf_op jit(solution)/shard_map/all_to_all | solution.py:34
  56.1 1.1 broadcast_in_dim.2
  57.1 0.0 copy-start
  57.1 0.0 copy-start.1
  57.1 3.7 %all-to-all-start.2 = ((bf16[8,64,896]{2,1,0:T(8,128)(2,1)}), bf16[8,64,896]{2,1,0:T(8,128)(2,1)S(1)}, u32[]{:S(2)}, u32[]{:S(2)}) async-start(bf16[8,64,896]{2,1,0:T(8,128)(2,1)} %broadcast_in_dim.2), calls=%async_computation.2 | async-start | bytes 1835008 | tf_op jit(solution)/shard_map/all_to_all | solution.py:34
  60.8 0.0 copy-done
  60.8 5.1 %collective-permute-start = (bf16[3584,128]{1,0:T(8,128)(2,1)S(1)}, bf16[3584,128]{1,0:T(8,128)(2,1)S(1)}, u32[]{:S(2)}, u32[]{:S(2)}) collective-permute-start(bf16[3584,128]{1,0:T(8,128)(2,1)S(1)} %bitcast.6), channel_id=1, source_target_pairs={{0,1},{1,0},{2,3},{3,2},{4,5},{5,4},{6,7},{7,6},{8,9},{9,8},{10,11... | collective-permute-start | bytes 2752520 | tf_op jit(solution)/shard_map/ppermute | solution.py:171
  66.0 0.0 copy-done.1
  66.0 1.9 %collective-permute-start.1 = (bf16[3584,128]{1,0:T(8,128)(2,1)S(1)}, bf16[3584,128]{1,0:T(8,128)(2,1)S(1)}, u32[]{:S(2)}, u32[]{:S(2)}) collective-permute-start(bf16[3584,128]{1,0:T(8,128)(2,1)S(1)} %bitcast.10), channel_id=1, source_target_pairs={{0,1},{1,0},{2,3},{3,2},{4,5},{5,4},{6,7},{7,6},{8,9},{9,8},{10,11... | collective-permute-start | bytes 2752520 | tf_op jit(solution)/shard_map/ppermute | solution.py:171
  67.9 2.4 %collective-permute-start.2 = (bf16[128,3584]{1,0:T(8,128)(2,1)}, bf16[128,3584]{1,0:T(8,128)(2,1)}, u32[]{:S(2)}, u32[]{:S(2)}) collective-permute-start(bf16[128,3584]{1,0:T(8,128)(2,1)} %bitcast.11), channel_id=1, source_target_pairs={{0,1},{1,0},{2,3},{3,2},{4,5},{5,4},{6,7},{7,6},{8,9},{9,8},{10,11... | collective-permute-start | bytes 2752520 | tf_op jit(solution)/shard_map/ppermute | solution.py:171
  70.3 0.0 collective-permute-done.refs_3_
  70.4 0.0 copy-start.2
  70.4 0.0 collective-permute-done.1.refs_4_
  70.4 0.9 copy-done.2
  71.3 0.0 copy-start.3
  71.3 0.9 copy-done.3
  72.3 0.5 collective-permute-done.2.refs_5_
  72.7 0.0 all-to-all-done.2.rows_ref
  72.7 4.4 %shard_map.88 = bf16[8,64,512]{2,1,0:T(8,128)(2,1)S(1)} custom-call(bf16[64,128]{1,0:T(8,128)(2,1)S(1)} %slice.8.aux_ref, bf16[8,64,896]{2,1,0:T(8,128)(2,1)S(1)} %all-to-all-done.2.rows_ref, bf16[3584,128]{1,0:T(8,128)(2,1)S(1)} %bitcast.7, bf16[3584,128]{1,0:T(8,128)(2,1)} %bitcast.9, bf16[128,3584]{1,0:T(8,128)(2,1)} %bitcast.12, ...), custom_call_target="tpu_custom_call" | custom-call | flops 587202560 | bytes 8388608 | tf_op jit(solution)/shard_map/pallas_call | solution.py:173
  77.2 13.9 %all_to_all.32 = bf16[8,64,512]{2,1,0:T(8,128)(2,1)S(1)} all-to-all(bf16[8,64,512]{2,1,0:T(8,128)(2,1)S(1)} %shard_map.88), channel_id=1, replica_groups=mesh['z'=16,'yh'=4,'yl'=2,'x'=4,'c'=2] {'yl','x'}, dimensions={0} | all-to-all | bytes 1048576 | tf_op jit(solution)/shard_map/all_to_all | solution.py:34
  91.1 0.1 reduce_sum.12
  91.2 17.6 %all_to_all.33 = bf16[16,4,512]{2,1,0:T(4,128)(2,1)S(1)} all-to-all(bf16[16,4,512]{2,1,0:T(4,128)(2,1)S(1)} %reshape.26), channel_id=1, replica_groups=mesh['z'=16,'yh'=4,'yl'=2,'x'=4,'c'=2] {'z'}, dimensions={0} | all-to-all | bytes 131072 | tf_op jit(solution)/shard_map/all_to_all | solution.py:34
  108.8 0.1 convolution_convert_fusion
  109.0 17.3 %all_to_all.34.home_ref = bf16[64,4,128]{2,1,0:T(4,128)(2,1)S(1)} all-to-all(bf16[64,4,128]{2,1,0:T(4,128)(2,1)S(1)} %reshape.28), channel_id=1, replica_groups=mesh['z'=16,'yh'=4,'yl'=2,'x'=4,'c'=2] {'yh','yl','x','c'}, dimensions={0} | all-to-all | bytes 131072 | tf_op jit(solution)/shard_map/all_to_all | solution.py:34
  126.3 0.6 shard_map.89
  (6 shorter events, 0.1 us)
Async XLA Ops:
  57.1 3.7 %copy-start = (bf16[1,3584,128]{2,1,0:T(8,128)(2,1)S(1)}, bf16[1,3584,128]{2,1,0:T(8,128)(2,1)}, u32[]{:S(2)}) copy-start(bf16[1,3584,128]{2,1,0:T(8,128)(2,1)} %param.11) | copy-start | bytes 2752516
  57.1 8.9 %copy-start.1 = (bf16[1,3584,128]{2,1,0:T(8,128)(2,1)S(1)}, bf16[1,3584,128]{2,1,0:T(8,128)(2,1)}, u32[]{:S(2)}) copy-start(bf16[1,3584,128]{2,1,0:T(8,128)(2,1)} %param.12) | copy-start | bytes 2752516
  57.1 15.6 %all-to-all-start.2 = ((bf16[8,64,896]{2,1,0:T(8,128)(2,1)}), bf16[8,64,896]{2,1,0:T(8,128)(2,1)S(1)}, u32[]{:S(2)}, u32[]{:S(2)}) async-start(bf16[8,64,896]{2,1,0:T(8,128)(2,1)} %broadcast_in_dim.2), calls=%async_computation.2 | async-start | bytes 1835008 | tf_op jit(solution)/shard_map/all_to_all | solution.py:34
  60.8 9.5 %collective-permute-start = (bf16[3584,128]{1,0:T(8,128)(2,1)S(1)}, bf16[3584,128]{1,0:T(8,128)(2,1)S(1)}, u32[]{:S(2)}, u32[]{:S(2)}) collective-permute-start(bf16[3584,128]{1,0:T(8,128)(2,1)S(1)} %bitcast.6), channel_id=1, source_target_pairs={{0,1},{1,0},{2,3},{3,2},{4,5},{5,4},{6,7},{7,6},{8,9},{9,8},{10,11... | collective-permute-start | bytes 2752520 | tf_op jit(solution)/shard_map/ppermute | solution.py:171
  66.0 4.4 %collective-permute-start.1 = (bf16[3584,128]{1,0:T(8,128)(2,1)S(1)}, bf16[3584,128]{1,0:T(8,128)(2,1)S(1)}, u32[]{:S(2)}, u32[]{:S(2)}) collective-permute-start(bf16[3584,128]{1,0:T(8,128)(2,1)S(1)} %bitcast.10), channel_id=1, source_target_pairs={{0,1},{1,0},{2,3},{3,2},{4,5},{5,4},{6,7},{7,6},{8,9},{9,8},{10,11... | collective-permute-start | bytes 2752520 | tf_op jit(solution)/shard_map/ppermute | solution.py:171
  67.9 4.8 %collective-permute-start.2 = (bf16[128,3584]{1,0:T(8,128)(2,1)}, bf16[128,3584]{1,0:T(8,128)(2,1)}, u32[]{:S(2)}, u32[]{:S(2)}) collective-permute-start(bf16[128,3584]{1,0:T(8,128)(2,1)} %bitcast.11), channel_id=1, source_target_pairs={{0,1},{1,0},{2,3},{3,2},{4,5},{5,4},{6,7},{7,6},{8,9},{9,8},{10,11... | collective-permute-start | bytes 2752520 | tf_op jit(solution)/shard_map/ppermute | solution.py:171
  70.4 1.0 copy-start.2
  71.3 0.9 copy-start.3

commit v6 on v5

--- a/solution.py
+++ b/solution.py
@@ -90,12 +90,15 @@
     for copy in copies:
         copy.start()
     column = 2 * lax.axis_index("yh") + lax.axis_index("yl")
-    rows = rows_ref.shape[1]
+    rows = aux_ref.shape[0]
     lane = lax.broadcasted_iota(jnp.int32, (rows, LANES), 1)
     prob = jnp.where(lane == column, aux_ref[...].astype(F32), 0.0)
     prob = jnp.sum(prob, axis=1, keepdims=True)
-    x = jnp.concatenate([rows_ref[i] for i in range(4)], axis=1)
-    dy = jnp.concatenate([rows_ref[i] for i in range(4, 8)], axis=1)
+    tiles = [
+        [rows_ref[q, k * rows : (k + 1) * rows, :] for k in range(TILES)] for q in range(8)
+    ]
+    x = jnp.concatenate(sum(tiles[:4], []), axis=1)
+    dy = jnp.concatenate(sum(tiles[4:], []), axis=1)
     gate_terms = jnp.zeros((rows, 1), F32)
     grads = []
     for core in range(2):
@@ -169,7 +172,8 @@
     rows = rows.reshape(slots, PIECE + LANES)
 
     others = [lax.ppermute(weight, "c", SWAP) for weight in weights]
-    own = exchange(jnp.broadcast_to(rows[None, :, :PIECE], (8, slots, PIECE)), QUAD)
+    tiles = rows[:, :PIECE].reshape(slots, TILES, LANES).transpose(1, 0, 2).reshape(TILES * slots, LANES)
+    own = exchange(jnp.broadcast_to(tiles[None], (8, TILES * slots, LANES)), QUAD)
     partial = pl.pallas_call(
         expert_kernel,
         out_shape=jax.ShapeDtypeStruct((8, slots, BACK), BF16),

time: 127 us -> 128 us (level)
  no operation moved by 1% of the time
where the time goes in v6:
time: 128 us; the launch traced here: 127 us
  blocking collectives  102 us (80%)
  starting transfers between devices  13.2 us (10%)
  Pallas kernels  7.1 us (6%)
  local copies, waits for them, and re-layouts  3.32 us (3%)
    all_to_all x5, blocking collectives, exchange(): return lax.all_to_all(value, axes, split_axis=0, concat_axis=0, tiled=True)  102 us
    ppermute x3, starting transfers between devices, on_device(): others = [lax.ppermute(weight, 'c', SWAP) for weight in weights]  9.47 us
    pallas_call x1, Pallas kernels, on_device(): pl.pallas_call(expert_kernel, out_shape=jax.ShapeDtypeStruct((8, slots, B...  4.43 us
    all_to_all x1, starting transfers between devices, exchange(): return lax.all_to_all(value, axes, split_axis=0, concat_axis=0, tiled=True)  3.68 us
  transfers between devices with their start and end apart: 4, of which 1 were waited for; matrix products, arithmetic and copies ran while one was open for 0% of the time, Pallas kernels for 0%

profile of v6, /device:TPU:1, one launch (start us, length us, event | category | flops | bytes accessed | tf_op | source)
XLA Modules:
  0.0 127.1 jit_solution(15576598046036374398)
XLA Ops:
  0.6 1.5 %shard_map.86 = bf16[64,8,128]{2,1,0:T(8,128)(2,1)} custom-call(bf16[1,3584]{1,0:T(2,128)(2,1)} %x_hbm.1, bf16[1,3584]{1,0:T(2,128)(2,1)} %dy_hbm.1, bf16[1,8]{1,0:T(2,128)(2,1)} %gate_hbm.1, s32[1,8]{1,0:T(1,128)} %dest_hbm.1), custom_call_target="tpu_custom_call" | custom-call | tf_op jit(solution)/shard_map/pallas_call | solution.py:144
  2.1 29.6 %all_to_all.30 = bf16[64,8,128]{2,1,0:T(8,128)(2,1)S(1)} all-to-all(bf16[64,8,128]{2,1,0:T(8,128)(2,1)} %shard_map.86), channel_id=1, replica_groups=mesh['z'=16,'yh'=4,'yl'=2,'x'=4,'c'=2] {'yh','yl','x','c'}, dimensions={0} | all-to-all | bytes 262144 | tf_op jit(solution)/shard_map/all_to_all | solution.py:34
  31.8 0.5 shard_map.87
  32.3 0.1 reshape.27
  32.3 23.7 %all_to_all.31 = bf16[16,4,1024]{2,1,0:T(4,128)(2,1)S(1)} all-to-all(bf16[16,4,1024]{2,1,0:T(4,128)(2,1)S(1)} %reshape.27), channel_id=1, replica_groups=mesh['z'=16,'yh'=4,'yl'=2,'x'=4,'c'=2] {'z'}, dimensions={0} | all-to-all | bytes 262144 | tf_op jit(solution)/shard_map/all_to_all | solution.py:34
  56.1 0.2 reshape.29
  56.2 1.1 broadcast_in_dim.8
  57.3 0.0 copy-start
  57.3 0.0 copy-start.1
  57.3 3.7 %all-to-all-start.2 = ((bf16[8,448,128]{2,1,0:T(8,128)(2,1)}), bf16[8,448,128]{2,1,0:T(8,128)(2,1)S(1)}, u32[]{:S(2)}, u32[]{:S(2)}) async-start(bf16[8,448,128]{2,1,0:T(8,128)(2,1)} %broadcast_in_dim.8), calls=%async_computation.2 | async-start | bytes 1835008 | tf_op jit(solution)/shard_map/all_to_all | solution.py:34
  61.0 0.0 copy-done
  61.0 5.1 %collective-permute-start = (bf16[3584,128]{1,0:T(8,128)(2,1)S(1)}, bf16[3584,128]{1,0:T(8,128)(2,1)S(1)}, u32[]{:S(2)}, u32[]{:S(2)}) collective-permute-start(bf16[3584,128]{1,0:T(8,128)(2,1)S(1)} %bitcast.8), channel_id=1, source_target_pairs={{0,1},{1,0},{2,3},{3,2},{4,5},{5,4},{6,7},{7,6},{8,9},{9,8},{10,11... | collective-permute-start | bytes 2752520 | tf_op jit(solution)/shard_map/ppermute | solution.py:174
  66.2 0.0 copy-done.1
  66.2 1.9 %collective-permute-start.1 = (bf16[3584,128]{1,0:T(8,128)(2,1)S(1)}, bf16[3584,128]{1,0:T(8,128)(2,1)S(1)}, u32[]{:S(2)}, u32[]{:S(2)}) collective-permute-start(bf16[3584,128]{1,0:T(8,128)(2,1)S(1)} %bitcast.12), channel_id=1, source_target_pairs={{0,1},{1,0},{2,3},{3,2},{4,5},{5,4},{6,7},{7,6},{8,9},{9,8},{10,11... | collective-permute-start | bytes 2752520 | tf_op jit(solution)/shard_map/ppermute | solution.py:174
  68.1 2.4 %collective-permute-start.2 = (bf16[128,3584]{1,0:T(8,128)(2,1)}, bf16[128,3584]{1,0:T(8,128)(2,1)}, u32[]{:S(2)}, u32[]{:S(2)}) collective-permute-start(bf16[128,3584]{1,0:T(8,128)(2,1)} %bitcast.13), channel_id=1, source_target_pairs={{0,1},{1,0},{2,3},{3,2},{4,5},{5,4},{6,7},{7,6},{8,9},{9,8},{10,11... | collective-permute-start | bytes 2752520 | tf_op jit(solution)/shard_map/ppermute | solution.py:174
  70.5 0.0 collective-permute-done.refs_3_
  70.5 0.0 copy-start.2
  70.5 0.0 collective-permute-done.1.refs_4_
  70.6 0.9 copy-done.2
  71.5 0.0 copy-start.3
  71.5 0.9 copy-done.3
  72.5 0.5 collective-permute-done.2.refs_5_
  72.9 0.0 all-to-all-done.2.rows_ref
  72.9 4.4 %shard_map.88 = bf16[8,64,512]{2,1,0:T(8,128)(2,1)S(1)} custom-call(bf16[64,128]{1,0:T(8,128)(2,1)S(1)} %slice.8.aux_ref, bf16[8,448,128]{2,1,0:T(8,128)(2,1)S(1)} %all-to-all-done.2.rows_ref, bf16[3584,128]{1,0:T(8,128)(2,1)S(1)} %bitcast.9, bf16[3584,128]{1,0:T(8,128)(2,1)} %bitcast.11, bf16[128,3584]{1,0:T(8,128)(2,1)} %bitcast.14, ...), custom_call_target="tpu_custom_call" | custom-call | flops 587202560 | bytes 8388608 | tf_op jit(solution)/shard_map/pallas_call | solution.py:177
  77.4 13.9 %all_to_all.32 = bf16[8,64,512]{2,1,0:T(8,128)(2,1)S(1)} all-to-all(bf16[8,64,512]{2,1,0:T(8,128)(2,1)S(1)} %shard_map.88), channel_id=1, replica_groups=mesh['z'=16,'yh'=4,'yl'=2,'x'=4,'c'=2] {'yl','x'}, dimensions={0} | all-to-all | bytes 1048576 | tf_op jit(solution)/shard_map/all_to_all | solution.py:34
  91.3 0.1 reduce_sum.12
  91.4 17.6 %all_to_all.33 = bf16[16,4,512]{2,1,0:T(4,128)(2,1)S(1)} all-to-all(bf16[16,4,512]{2,1,0:T(4,128)(2,1)S(1)} %reshape.30), channel_id=1, replica_groups=mesh['z'=16,'yh'=4,'yl'=2,'x'=4,'c'=2] {'z'}, dimensions={0} | all-to-all | bytes 131072 | tf_op jit(solution)/shard_map/all_to_all | solution.py:34
  109.0 0.1 convolution_convert_fusion
  109.2 17.3 %all_to_all.34.home_ref = bf16[64,4,128]{2,1,0:T(4,128)(2,1)S(1)} all-to-all(bf16[64,4,128]{2,1,0:T(4,128)(2,1)S(1)} %reshape.32), channel_id=1, replica_groups=mesh['z'=16,'yh'=4,'yl'=2,'x'=4,'c'=2] {'yh','yl','x','c'}, dimensions={0} | all-to-all | bytes 131072 | tf_op jit(solution)/shard_map/all_to_all | solution.py:34
  126.5 0.6 shard_map.89
  (7 shorter events, 0.1 us)
Async XLA Ops:
  57.3 3.7 %copy-start = (bf16[1,3584,128]{2,1,0:T(8,128)(2,1)S(1)}, bf16[1,3584,128]{2,1,0:T(8,128)(2,1)}, u32[]{:S(2)}) copy-start(bf16[1,3584,128]{2,1,0:T(8,128)(2,1)} %param.11) | copy-start | bytes 2752516
  57.3 8.9 %copy-start.1 = (bf16[1,3584,128]{2,1,0:T(8,128)(2,1)S(1)}, bf16[1,3584,128]{2,1,0:T(8,128)(2,1)}, u32[]{:S(2)}) copy-start(bf16[1,3584,128]{2,1,0:T(8,128)(2,1)} %param.12) | copy-start | bytes 2752516
  57.3 15.6 %all-to-all-start.2 = ((bf16[8,448,128]{2,1,0:T(8,128)(2,1)}), bf16[8,448,128]{2,1,0:T(8,128)(2,1)S(1)}, u32[]{:S(2)}, u32[]{:S(2)}) async-start(bf16[8,448,128]{2,1,0:T(8,128)(2,1)} %broadcast_in_dim.8), calls=%async_computation.2 | async-start | bytes 1835008 | tf_op jit(solution)/shard_map/all_to_all | solution.py:34
  61.0 9.5 %collective-permute-start = (bf16[3584,128]{1,0:T(8,128)(2,1)S(1)}, bf16[3584,128]{1,0:T(8,128)(2,1)S(1)}, u32[]{:S(2)}, u32[]{:S(2)}) collective-permute-start(bf16[3584,128]{1,0:T(8,128)(2,1)S(1)} %bitcast.8), channel_id=1, source_target_pairs={{0,1},{1,0},{2,3},{3,2},{4,5},{5,4},{6,7},{7,6},{8,9},{9,8},{10,11... | collective-permute-start | bytes 2752520 | tf_op jit(solution)/shard_map/ppermute | solution.py:174
  66.2 4.4 %collective-permute-start.1 = (bf16[3584,128]{1,0:T(8,128)(2,1)S(1)}, bf16[3584,128]{1,0:T(8,128)(2,1)S(1)}, u32[]{:S(2)}, u32[]{:S(2)}) collective-permute-start(bf16[3584,128]{1,0:T(8,128)(2,1)S(1)} %bitcast.12), channel_id=1, source_target_pairs={{0,1},{1,0},{2,3},{3,2},{4,5},{5,4},{6,7},{7,6},{8,9},{9,8},{10,11... | collective-permute-start | bytes 2752520 | tf_op jit(solution)/shard_map/ppermute | solution.py:174
  68.1 4.8 %collective-permute-start.2 = (bf16[128,3584]{1,0:T(8,128)(2,1)}, bf16[128,3584]{1,0:T(8,128)(2,1)}, u32[]{:S(2)}, u32[]{:S(2)}) collective-permute-start(bf16[128,3584]{1,0:T(8,128)(2,1)} %bitcast.13), channel_id=1, source_target_pairs={{0,1},{1,0},{2,3},{3,2},{4,5},{5,4},{6,7},{7,6},{8,9},{9,8},{10,11... | collective-permute-start | bytes 2752520 | tf_op jit(solution)/shard_map/ppermute | solution.py:174
  70.5 1.0 copy-start.2
  71.5 0.9 copy-start.3

commit v7 on v5

--- a/solution.py
+++ b/solution.py
@@ -8,7 +8,7 @@
 
 AXES = ("z", "yh", "yl", "x", "c")
 LOCAL = ("yh", "yl", "x", "c")
-QUAD = ("yl", "x")
+QUAD = ("x", "yl")
 SWAP = ((0, 1), (1, 0))
 F32 = jnp.float32
 BF16 = jnp.bfloat16
@@ -32,6 +32,10 @@
 
 def exchange(value, axes):
     return lax.all_to_all(value, axes, split_axis=0, concat_axis=0, tiled=True)
+
+
+def quad_of(piece):
+    return piece % 4 * 2 + piece // 4
 
 
 def pack_kernel(x_hbm, dy_hbm, gate_hbm, dest_hbm, out_ref, x_ref, dy_ref, gate_ref, dest_ref, arrived):
@@ -94,8 +98,8 @@
     lane = lax.broadcasted_iota(jnp.int32, (rows, LANES), 1)
     prob = jnp.where(lane == column, aux_ref[...].astype(F32), 0.0)
     prob = jnp.sum(prob, axis=1, keepdims=True)
-    x = jnp.concatenate([rows_ref[i] for i in range(4)], axis=1)
-    dy = jnp.concatenate([rows_ref[i] for i in range(4, 8)], axis=1)
+    x = jnp.concatenate([rows_ref[quad_of(q)] for q in range(4)], axis=1)
+    dy = jnp.concatenate([rows_ref[quad_of(q)] for q in range(4, 8)], axis=1)
     gate_terms = jnp.zeros((rows, 1), F32)
     grads = []
     for core in range(2):
@@ -115,9 +119,9 @@
     for q in range(7):
         at = slice(q * BACK, (q + 1) * BACK)
         wide = [weights[i][at, :] for i in (0, 1, 3, 4)]
-        out_ref[q] = dot(grad, jnp.concatenate(wide, axis=1), NT).astype(BF16)
+        out_ref[quad_of(q)] = dot(grad, jnp.concatenate(wide, axis=1), NT).astype(BF16)
     lane = lax.broadcasted_iota(jnp.int32, (rows, BACK), 1)
-    out_ref[7] = jnp.where(lane == column, gate_terms, 0.0).astype(BF16)
+    out_ref[quad_of(7)] = jnp.where(lane == column, gate_terms, 0.0).astype(BF16)
 
 
 def sum_kernel(home_ref, grad_ref, gate_ref):

time: 127 us -> 127 us (level)
  no operation moved by 1% of the time
where the time goes in v7:
time: 127 us
  blocking collectives  102 us (80%)
  starting transfers between devices  13.2 us (10%)
  Pallas kernels  7.1 us (6%)
  local copies, waits for them, and re-layouts  3.14 us (2%)
    all_to_all x5, blocking collectives, exchange(): return lax.all_to_all(value, axes, split_axis=0, concat_axis=0, tiled=True)  102 us
    ppermute x3, starting transfers between devices, on_device(): others = [lax.ppermute(weight, 'c', SWAP) for weight in weights]  9.47 us
    pallas_call x1, Pallas kernels, on_device(): pl.pallas_call(expert_kernel, out_shape=jax.ShapeDtypeStruct((8, slots, B...  4.44 us
    all_to_all x1, starting transfers between devices, exchange(): return lax.all_to_all(value, axes, split_axis=0, concat_axis=0, tiled=True)  3.68 us
  transfers between devices with their start and end apart: 4, of which 1 were waited for; matrix products, arithmetic and copies ran while one was open for 0% of the time, Pallas kernels for 0%

profile of v7, /device:TPU:1, one launch (start us, length us, event | category | flops | bytes accessed | tf_op | source)
XLA Modules:
  0.0 126.9 jit_solution(9449330662533298464)
XLA Ops:
  0.6 1.5 %shard_map.86 = bf16[64,8,128]{2,1,0:T(8,128)(2,1)} custom-call(bf16[1,3584]{1,0:T(2,128)(2,1)} %x_hbm.1, bf16[1,3584]{1,0:T(2,128)(2,1)} %dy_hbm.1, bf16[1,8]{1,0:T(2,128)(2,1)} %gate_hbm.1, s32[1,8]{1,0:T(1,128)} %dest_hbm.1), custom_call_target="tpu_custom_call" | custom-call | tf_op jit(solution)/shard_map/pallas_call | solution.py:145
  2.1 29.6 %all_to_all.30 = bf16[64,8,128]{2,1,0:T(8,128)(2,1)S(1)} all-to-all(bf16[64,8,128]{2,1,0:T(8,128)(2,1)} %shard_map.86), channel_id=1, replica_groups=mesh['z'=16,'yh'=4,'yl'=2,'x'=4,'c'=2] {'yh','yl','x','c'}, dimensions={0} | all-to-all | bytes 262144 | tf_op jit(solution)/shard_map/all_to_all | solution.py:34
  31.8 0.5 shard_map.87
  32.3 0.1 reshape.24
  32.3 23.7 %all_to_all.31 = bf16[16,4,1024]{2,1,0:T(4,128)(2,1)S(1)} all-to-all(bf16[16,4,1024]{2,1,0:T(4,128)(2,1)S(1)} %reshape.24), channel_id=1, replica_groups=mesh['z'=16,'yh'=4,'yl'=2,'x'=4,'c'=2] {'z'}, dimensions={0} | all-to-all | bytes 262144 | tf_op jit(solution)/shard_map/all_to_all | solution.py:34
  56.1 1.1 broadcast_in_dim.2
  57.1 0.0 copy-start
  57.1 0.0 copy-start.1
  57.1 3.7 %all-to-all-start.2 = ((bf16[8,64,896]{2,1,0:T(8,128)(2,1)}), bf16[8,64,896]{2,1,0:T(8,128)(2,1)S(1)}, u32[]{:S(2)}, u32[]{:S(2)}) async-start(bf16[8,64,896]{2,1,0:T(8,128)(2,1)} %broadcast_in_dim.2), calls=%async_computation.2 | async-start | bytes 1835008 | tf_op jit(solution)/shard_map/all_to_all | solution.py:34
  60.8 0.0 copy-done
  60.8 5.1 %collective-permute-start = (bf16[3584,128]{1,0:T(8,128)(2,1)S(1)}, bf16[3584,128]{1,0:T(8,128)(2,1)S(1)}, u32[]{:S(2)}, u32[]{:S(2)}) collective-permute-start(bf16[3584,128]{1,0:T(8,128)(2,1)S(1)} %bitcast.6), channel_id=1, source_target_pairs={{0,1},{1,0},{2,3},{3,2},{4,5},{5,4},{6,7},{7,6},{8,9},{9,8},{10,11... | collective-permute-start | bytes 2752520 | tf_op jit(solution)/shard_map/ppermute | solution.py:175
  66.0 0.0 copy-done.1
  66.0 1.9 %collective-permute-start.1 = (bf16[3584,128]{1,0:T(8,128)(2,1)S(1)}, bf16[3584,128]{1,0:T(8,128)(2,1)S(1)}, u32[]{:S(2)}, u32[]{:S(2)}) collective-permute-start(bf16[3584,128]{1,0:T(8,128)(2,1)S(1)} %bitcast.10), channel_id=1, source_target_pairs={{0,1},{1,0},{2,3},{3,2},{4,5},{5,4},{6,7},{7,6},{8,9},{9,8},{10,11... | collective-permute-start | bytes 2752520 | tf_op jit(solution)/shard_map/ppermute | solution.py:175
  67.9 2.4 %collective-permute-start.2 = (bf16[128,3584]{1,0:T(8,128)(2,1)}, bf16[128,3584]{1,0:T(8,128)(2,1)}, u32[]{:S(2)}, u32[]{:S(2)}) collective-permute-start(bf16[128,3584]{1,0:T(8,128)(2,1)} %bitcast.11), channel_id=1, source_target_pairs={{0,1},{1,0},{2,3},{3,2},{4,5},{5,4},{6,7},{7,6},{8,9},{9,8},{10,11... | collective-permute-start | bytes 2752520 | tf_op jit(solution)/shard_map/ppermute | solution.py:175
  70.3 0.0 collective-permute-done.refs_3_
  70.4 0.0 copy-start.2
  70.4 0.0 collective-permute-done.1.refs_4_
  70.4 0.9 copy-done.2
  71.3 0.0 copy-start.3
  71.3 0.9 copy-done.3
  72.3 0.5 collective-permute-done.2.refs_5_
  72.7 0.0 all-to-all-done.2.rows_ref
  72.7 4.4 %shard_map.88 = bf16[8,64,512]{2,1,0:T(8,128)(2,1)S(1)} custom-call(bf16[64,128]{1,0:T(8,128)(2,1)S(1)} %slice.8.aux_ref, bf16[8,64,896]{2,1,0:T(8,128)(2,1)S(1)} %all-to-all-done.2.rows_ref, bf16[3584,128]{1,0:T(8,128)(2,1)S(1)} %bitcast.7, bf16[3584,128]{1,0:T(8,128)(2,1)} %bitcast.9, bf16[128,3584]{1,0:T(8,128)(2,1)} %bitcast.12, ...), custom_call_target="tpu_custom_call" | custom-call | flops 587202560 | bytes 8388608 | tf_op jit(solution)/shard_map/pallas_call | solution.py:177
  77.2 14.3 %all_to_all.32 = bf16[8,64,512]{2,1,0:T(8,128)(2,1)S(1)} all-to-all(bf16[8,64,512]{2,1,0:T(8,128)(2,1)S(1)} %shard_map.88), channel_id=1, replica_groups=mesh['z'=16,'yh'=4,'yl'=2,'x'=4,'c'=2] {'x','yl'}, dimensions={0} | all-to-all | bytes 1048576 | tf_op jit(solution)/shard_map/all_to_all | solution.py:34
  91.5 0.1 reduce_sum.12
  91.6 17.7 %all_to_all.33 = bf16[16,4,512]{2,1,0:T(4,128)(2,1)S(1)} all-to-all(bf16[16,4,512]{2,1,0:T(4,128)(2,1)S(1)} %reshape.26), channel_id=1, replica_groups=mesh['z'=16,'yh'=4,'yl'=2,'x'=4,'c'=2] {'z'}, dimensions={0} | all-to-all | bytes 131072 | tf_op jit(solution)/shard_map/all_to_all | solution.py:34
  109.3 0.1 convolution_convert_fusion
  109.5 16.8 %all_to_all.34.home_ref = bf16[64,4,128]{2,1,0:T(4,128)(2,1)S(1)} all-to-all(bf16[64,4,128]{2,1,0:T(4,128)(2,1)S(1)} %reshape.28), channel_id=1, replica_groups=mesh['z'=16,'yh'=4,'yl'=2,'x'=4,'c'=2] {'yh','yl','x','c'}, dimensions={0} | all-to-all | bytes 131072 | tf_op jit(solution)/shard_map/all_to_all | solution.py:34
  126.3 0.6 shard_map.89
  (6 shorter events, 0.1 us)
Async XLA Ops:
  57.1 3.7 %copy-start = (bf16[1,3584,128]{2,1,0:T(8,128)(2,1)S(1)}, bf16[1,3584,128]{2,1,0:T(8,128)(2,1)}, u32[]{:S(2)}) copy-start(bf16[1,3584,128]{2,1,0:T(8,128)(2,1)} %param.11) | copy-start | bytes 2752516
  57.1 8.9 %copy-start.1 = (bf16[1,3584,128]{2,1,0:T(8,128)(2,1)S(1)}, bf16[1,3584,128]{2,1,0:T(8,128)(2,1)}, u32[]{:S(2)}) copy-start(bf16[1,3584,128]{2,1,0:T(8,128)(2,1)} %param.12) | copy-start | bytes 2752516
  57.1 15.6 %all-to-all-start.2 = ((bf16[8,64,896]{2,1,0:T(8,128)(2,1)}), bf16[8,64,896]{2,1,0:T(8,128)(2,1)S(1)}, u32[]{:S(2)}, u32[]{:S(2)}) async-start(bf16[8,64,896]{2,1,0:T(8,128)(2,1)} %broadcast_in_dim.2), calls=%async_computation.2 | async-start | bytes 1835008 | tf_op jit(solution)/shard_map/all_to_all | solution.py:34
  60.8 9.5 %collective-permute-start = (bf16[3584,128]{1,0:T(8,128)(2,1)S(1)}, bf16[3584,128]{1,0:T(8,128)(2,1)S(1)}, u32[]{:S(2)}, u32[]{:S(2)}) collective-permute-start(bf16[3584,128]{1,0:T(8,128)(2,1)S(1)} %bitcast.6), channel_id=1, source_target_pairs={{0,1},{1,0},{2,3},{3,2},{4,5},{5,4},{6,7},{7,6},{8,9},{9,8},{10,11... | collective-permute-start | bytes 2752520 | tf_op jit(solution)/shard_map/ppermute | solution.py:175
  66.0 4.4 %collective-permute-start.1 = (bf16[3584,128]{1,0:T(8,128)(2,1)S(1)}, bf16[3584,128]{1,0:T(8,128)(2,1)S(1)}, u32[]{:S(2)}, u32[]{:S(2)}) collective-permute-start(bf16[3584,128]{1,0:T(8,128)(2,1)S(1)} %bitcast.10), channel_id=1, source_target_pairs={{0,1},{1,0},{2,3},{3,2},{4,5},{5,4},{6,7},{7,6},{8,9},{9,8},{10,11... | collective-permute-start | bytes 2752520 | tf_op jit(solution)/shard_map/ppermute | solution.py:175
  67.9 4.8 %collective-permute-start.2 = (bf16[128,3584]{1,0:T(8,128)(2,1)}, bf16[128,3584]{1,0:T(8,128)(2,1)}, u32[]{:S(2)}, u32[]{:S(2)}) collective-permute-start(bf16[128,3584]{1,0:T(8,128)(2,1)} %bitcast.11), channel_id=1, source_target_pairs={{0,1},{1,0},{2,3},{3,2},{4,5},{5,4},{6,7},{7,6},{8,9},{9,8},{10,11... | collective-permute-start | bytes 2752520 | tf_op jit(solution)/shard_map/ppermute | solution.py:175
  70.4 1.0 copy-start.2
  71.3 0.9 copy-start.3

commit v8 on v5

--- a/solution.py
+++ b/solution.py
@@ -79,6 +79,17 @@
     for k in range(TILES + 1):
         part = wide[pl.ds(k, tokens, stride=8), :].astype(BF16)
         send_ref[:, k * LANES : (k + 1) * LANES] = dot(place, part, TN).astype(BF16)
+
+
+def spread_kernel(rows_ref, out_ref, aux_ref, arrived):
+    copies = [
+        pltpu.make_async_copy(rows_ref.at[:, :PIECE], out_ref.at[i], arrived.at[i]) for i in range(8)
+    ]
+    for copy in copies:
+        copy.start()
+    aux_ref[...] = rows_ref[:, PIECE:]
+    for copy in copies:
+        copy.wait()
 
 
 def expert_kernel(aux_ref, rows_ref, *refs):
@@ -169,7 +180,18 @@
     rows = rows.reshape(slots, PIECE + LANES)
 
     others = [lax.ppermute(weight, "c", SWAP) for weight in weights]
-    own = exchange(jnp.broadcast_to(rows[None, :, :PIECE], (8, slots, PIECE)), QUAD)
+    spread, aux = pl.pallas_call(
+        spread_kernel,
+        out_shape=(
+            jax.ShapeDtypeStruct((8, slots, PIECE), BF16),
+            jax.ShapeDtypeStruct((slots, LANES), BF16),
+        ),
+        in_specs=[VMEM],
+        out_specs=(HBM, VMEM),
+        scratch_shapes=[pltpu.SemaphoreType.DMA((8,))],
+        compiler_params=pltpu.CompilerParams(vmem_limit_bytes=4 * MIB),
+    )(rows)
+    own = exchange(spread, QUAD)
     partial = pl.pallas_call(
         expert_kernel,
         out_shape=jax.ShapeDtypeStruct((8, slots, BACK), BF16),
@@ -185,7 +207,7 @@
             bytes_accessed=8 * MIB,
             transcendentals=2 * slots * LANES,
         ),
-    )(rows[:, PIECE:], own, *weights, *others)
+    )(aux, own, *weights, *others)
 
     terms = exchange(partial, QUAD)
     summed = jnp.sum(terms.astype(F32), axis=0).astype(BF16)

time: 127 us -> 127 us (level)
  no operation moved by 1% of the time
where the time goes in v8:
time: 127 us
  blocking collectives  102 us (80%)
  starting transfers between devices  13.2 us (10%)
  Pallas kernels  8.11 us (6%)
  local copies, waits for them, and re-layouts  2.07 us (2%)
    all_to_all x5, blocking collectives, exchange(): return lax.all_to_all(value, axes, split_axis=0, concat_axis=0, tiled=True)  102 us
    ppermute x3, starting transfers between devices, on_device(): others = [lax.ppermute(weight, 'c', SWAP) for weight in weights]  9.47 us
    pallas_call x1, Pallas kernels, on_device(): pl.pallas_call(expert_kernel, out_shape=jax.ShapeDtypeStruct((8, slots, B...  4.43 us
    all_to_all x1, starting transfers between devices, exchange(): return lax.all_to_all(value, axes, split_axis=0, concat_axis=0, tiled=True)  3.7 us
  transfers between devices with their start and end apart: 4, of which 1 were waited for; matrix products, arithmetic and copies ran while one was open for 0% of the time, Pallas kernels for 0%

profile of v8, /device:TPU:1, one launch (start us, length us, event | category | flops | bytes accessed | tf_op | source)
XLA Modules:
  0.0 126.9 jit_solution(8762176378757134374)
XLA Ops:
  0.6 1.5 %shard_map.86 = bf16[64,8,128]{2,1,0:T(8,128)(2,1)} custom-call(bf16[1,3584]{1,0:T(2,128)(2,1)} %x_hbm.1, bf16[1,3584]{1,0:T(2,128)(2,1)} %dy_hbm.1, bf16[1,8]{1,0:T(2,128)(2,1)} %gate_hbm.1, s32[1,8]{1,0:T(1,128)} %dest_hbm.1), custom_call_target="tpu_custom_call" | custom-call | tf_op jit(solution)/shard_map/pallas_call | solution.py:152
  2.1 29.6 %all_to_all.30 = bf16[64,8,128]{2,1,0:T(8,128)(2,1)S(1)} all-to-all(bf16[64,8,128]{2,1,0:T(8,128)(2,1)} %shard_map.86), channel_id=1, replica_groups=mesh['z'=16,'yh'=4,'yl'=2,'x'=4,'c'=2] {'yh','yl','x','c'}, dimensions={0} | all-to-all | bytes 262144 | tf_op jit(solution)/shard_map/all_to_all | solution.py:34
  31.8 0.5 shard_map.87
  32.3 0.1 reshape.23
  32.4 23.6 %all_to_all.31 = bf16[16,4,1024]{2,1,0:T(4,128)(2,1)S(1)} all-to-all(bf16[16,4,1024]{2,1,0:T(4,128)(2,1)S(1)} %reshape.23), channel_id=1, replica_groups=mesh['z'=16,'yh'=4,'yl'=2,'x'=4,'c'=2] {'z'}, dimensions={0} | all-to-all | bytes 262144 | tf_op jit(solution)/shard_map/all_to_all | solution.py:34
  56.0 1.0 shard_map.88
  57.1 0.0 copy-start
  57.1 0.0 copy-start.1
  57.1 3.7 %all-to-all-start.2 = ((bf16[8,64,896]{2,1,0:T(8,128)(2,1)}), bf16[8,64,896]{2,1,0:T(8,128)(2,1)S(1)}, u32[]{:S(2)}, u32[]{:S(2)}) async-start(bf16[8,64,896]{2,1,0:T(8,128)(2,1)} %get-tuple-element.9), calls=%async_computation.2 | async-start | bytes 1835008 | tf_op jit(solution)/shard_map/all_to_all | solution.py:34
  60.8 0.0 copy-done
  60.8 5.1 %collective-permute-start = (bf16[3584,128]{1,0:T(8,128)(2,1)S(1)}, bf16[3584,128]{1,0:T(8,128)(2,1)S(1)}, u32[]{:S(2)}, u32[]{:S(2)}) collective-permute-start(bf16[3584,128]{1,0:T(8,128)(2,1)S(1)} %bitcast.6), channel_id=1, source_target_pairs={{0,1},{1,0},{2,3},{3,2},{4,5},{5,4},{6,7},{7,6},{8,9},{9,8},{10,11... | collective-permute-start | bytes 2752520 | tf_op jit(solution)/shard_map/ppermute | solution.py:182
  65.9 0.0 copy-done.1
  66.0 1.9 %collective-permute-start.1 = (bf16[3584,128]{1,0:T(8,128)(2,1)S(1)}, bf16[3584,128]{1,0:T(8,128)(2,1)S(1)}, u32[]{:S(2)}, u32[]{:S(2)}) collective-permute-start(bf16[3584,128]{1,0:T(8,128)(2,1)S(1)} %bitcast.10), channel_id=1, source_target_pairs={{0,1},{1,0},{2,3},{3,2},{4,5},{5,4},{6,7},{7,6},{8,9},{9,8},{10,11... | collective-permute-start | bytes 2752520 | tf_op jit(solution)/shard_map/ppermute | solution.py:182
  67.9 2.4 %collective-permute-start.2 = (bf16[128,3584]{1,0:T(8,128)(2,1)}, bf16[128,3584]{1,0:T(8,128)(2,1)}, u32[]{:S(2)}, u32[]{:S(2)}) collective-permute-start(bf16[128,3584]{1,0:T(8,128)(2,1)} %bitcast.11), channel_id=1, source_target_pairs={{0,1},{1,0},{2,3},{3,2},{4,5},{5,4},{6,7},{7,6},{8,9},{9,8},{10,11... | collective-permute-start | bytes 2752520 | tf_op jit(solution)/shard_map/ppermute | solution.py:182
  70.3 0.0 collective-permute-done.refs_3_
  70.3 0.0 copy-start.2
  70.3 0.0 collective-permute-done.1.refs_4_
  70.3 0.9 copy-done.2
  71.3 0.0 copy-start.3
  71.3 1.0 copy-done.3
  72.2 0.5 collective-permute-done.2.refs_5_
  72.7 0.0 all-to-all-done.2.rows_ref
  72.7 4.4 %shard_map.89 = bf16[8,64,512]{2,1,0:T(8,128)(2,1)S(1)} custom-call(bf16[64,128]{1,0:T(8,128)(2,1)S(1)} %get-tuple-element.8.aux_ref, bf16[8,64,896]{2,1,0:T(8,128)(2,1)S(1)} %all-to-all-done.2.rows_ref, bf16[3584,128]{1,0:T(8,128)(2,1)S(1)} %bitcast.7, bf16[3584,128]{1,0:T(8,128)(2,1)} %bitcast.9, bf16[128,3584]{1,0:T(8,128)(2,1)} %bitcast.12, ...), custom_call_target="tpu_custom_call" | custom-call | flops 587202560 | bytes 8388608 | tf_op jit(solution)/shard_map/pallas_call | solution.py:195
  77.2 14.0 %all_to_all.32 = bf16[8,64,512]{2,1,0:T(8,128)(2,1)S(1)} all-to-all(bf16[8,64,512]{2,1,0:T(8,128)(2,1)S(1)} %shard_map.89), channel_id=1, replica_groups=mesh['z'=16,'yh'=4,'yl'=2,'x'=4,'c'=2] {'yl','x'}, dimensions={0} | all-to-all | bytes 1048576 | tf_op jit(solution)/shard_map/all_to_all | solution.py:34
  91.1 0.1 reduce_sum.12
  91.2 17.6 %all_to_all.33 = bf16[16,4,512]{2,1,0:T(4,128)(2,1)S(1)} all-to-all(bf16[16,4,512]{2,1,0:T(4,128)(2,1)S(1)} %reshape.25), channel_id=1, replica_groups=mesh['z'=16,'yh'=4,'yl'=2,'x'=4,'c'=2] {'z'}, dimensions={0} | all-to-all | bytes 131072 | tf_op jit(solution)/shard_map/all_to_all | solution.py:34
  108.8 0.1 convolution_convert_fusion
  109.0 17.3 %all_to_all.34.home_ref = bf16[64,4,128]{2,1,0:T(4,128)(2,1)S(1)} all-to-all(bf16[64,4,128]{2,1,0:T(4,128)(2,1)S(1)} %reshape.27), channel_id=1, replica_groups=mesh['z'=16,'yh'=4,'yl'=2,'x'=4,'c'=2] {'yh','yl','x','c'}, dimensions={0} | all-to-all | bytes 131072 | tf_op jit(solution)/shard_map/all_to_all | solution.py:34
  126.3 0.6 shard_map.90
  (4 shorter events, 0.1 us)
Async XLA Ops:
  57.1 3.7 %copy-start = (bf16[1,3584,128]{2,1,0:T(8,128)(2,1)S(1)}, bf16[1,3584,128]{2,1,0:T(8,128)(2,1)}, u32[]{:S(2)}) copy-start(bf16[1,3584,128]{2,1,0:T(8,128)(2,1)} %param.11) | copy-start | bytes 2752516
  57.1 8.9 %copy-start.1 = (bf16[1,3584,128]{2,1,0:T(8,128)(2,1)S(1)}, bf16[1,3584,128]{2,1,0:T(8,128)(2,1)}, u32[]{:S(2)}) copy-start(bf16[1,3584,128]{2,1,0:T(8,128)(2,1)} %param.12) | copy-start | bytes 2752516
  57.1 15.6 %all-to-all-start.2 = ((bf16[8,64,896]{2,1,0:T(8,128)(2,1)}), bf16[8,64,896]{2,1,0:T(8,128)(2,1)S(1)}, u32[]{:S(2)}, u32[]{:S(2)}) async-start(bf16[8,64,896]{2,1,0:T(8,128)(2,1)} %get-tuple-element.9), calls=%async_computation.2 | async-start | bytes 1835008 | tf_op jit(solution)/shard_map/all_to_all | solution.py:34
  60.8 9.5 %collective-permute-start = (bf16[3584,128]{1,0:T(8,128)(2,1)S(1)}, bf16[3584,128]{1,0:T(8,128)(2,1)S(1)}, u32[]{:S(2)}, u32[]{:S(2)}) collective-permute-start(bf16[3584,128]{1,0:T(8,128)(2,1)S(1)} %bitcast.6), channel_id=1, source_target_pairs={{0,1},{1,0},{2,3},{3,2},{4,5},{5,4},{6,7},{7,6},{8,9},{9,8},{10,11... | collective-permute-start | bytes 2752520 | tf_op jit(solution)/shard_map/ppermute | solution.py:182
  66.0 4.4 %collective-permute-start.1 = (bf16[3584,128]{1,0:T(8,128)(2,1)S(1)}, bf16[3584,128]{1,0:T(8,128)(2,1)S(1)}, u32[]{:S(2)}, u32[]{:S(2)}) collective-permute-start(bf16[3584,128]{1,0:T(8,128)(2,1)S(1)} %bitcast.10), channel_id=1, source_target_pairs={{0,1},{1,0},{2,3},{3,2},{4,5},{5,4},{6,7},{7,6},{8,9},{9,8},{10,11... | collective-permute-start | bytes 2752520 | tf_op jit(solution)/shard_map/ppermute | solution.py:182
  67.9 4.8 %collective-permute-start.2 = (bf16[128,3584]{1,0:T(8,128)(2,1)}, bf16[128,3584]{1,0:T(8,128)(2,1)}, u32[]{:S(2)}, u32[]{:S(2)}) collective-permute-start(bf16[128,3584]{1,0:T(8,128)(2,1)} %bitcast.11), channel_id=1, source_target_pairs={{0,1},{1,0},{2,3},{3,2},{4,5},{5,4},{6,7},{7,6},{8,9},{9,8},{10,11... | collective-permute-start | bytes 2752520 | tf_op jit(solution)/shard_map/ppermute | solution.py:182
  70.3 1.0 copy-start.2
  71.3 1.0 copy-start.3
